TPU v7x, 128 devices: a whole 4x4x4 slice. The times are simulated.
128 devices in a mesh: dp: 4 (over y), seq: 32 (over z, x, core).
Axes of the slice: x: 4, y: 4, z: 4, core: 2. Of those that a mesh axis runs over, the one named last changes fastest.
Arguments:
- query: bfloat16 [16384, 3072], P(('dp', 'seq')), parts along dimension 0, may hold values from -24 to 24
- key_in: bfloat16 [16384, 3072], P(('dp', 'seq')), parts along dimension 0, may hold values from -24 to 24
- value: bfloat16 [16384, 3072], P(('dp', 'seq')), parts along dimension 0, may hold values from -6 to 6
- grad_out: bfloat16 [16384, 3072], P(('dp', 'seq')), parts along dimension 0, may hold values from -6 to 6
- masks: int32 [96, 32, 32], P('dp'), parts along dimension 0, may hold values from 0 to 1, as said below
Outputs:
- attn_out: bfloat16 [16384, 3072], P(('dp', 'seq')), parts along dimension 0
- grad_query: bfloat16 [16384, 3072], P(('dp', 'seq')), parts along dimension 0
- grad_key: bfloat16 [16384, 3072], P(('dp', 'seq')), parts along dimension 0
- grad_value: bfloat16 [16384, 3072], P(('dp', 'seq')), parts along dimension 0
There are 4 independent parts, one for each index of `dp`. A program takes and returns all parts, laid end to end along the dimension named above; each array names one. Nothing has to cross between parts.
Inputs may be any that keep to these rules, and one draw needn't show every extreme that they name: masks[h, i, i] is 1 for every head h and block i.
All inputs are finite; a program needn't handle non-finite values.
Results may differ from a plain program's by a relative error of at most 0.012.
Values may be sent and summed in bfloat16 or wider, within the bound.
No kernel may reach another device: no remote copies, remote signals or barrier semaphores. Data moves between devices by JAX's collectives and lax.ppermute only.
A program may use at most 128 MiB of HBM per device.

v0:
```python
import functools

import jax
import jax.numpy as jnp
from jax import lax
from jax.experimental import pallas as pl
from jax.experimental.pallas import tpu as pltpu
from jax.sharding import PartitionSpec as P

LANES = 512
BLOCK = 256
STEP = 2048
NT = (((1,), (1,)), ((), ()))
NN = (((1,), (0,)), ((), ()))
LOG2E = 1.4426950408889634


def at_multiple(x, n):
    return x if isinstance(x, int) else pl.multiple_of(x, n)


def dense_kernel(block, step_rows, lanes, split, masks_ref, own_ref, oth_ref, *refs):
    (rows_ref, give_ref,
    k_scr, v_scr, kt_scr, vt_scr, dk_scr, dv_scr, x_scr, p_scr, bias_ref, mask_scr, sem) = refs[-13:]
    half, slots, tile, width = own_ref.shape
    keys = 2 * half * tile
    queries = half * tile // (2 if split else 1)
    tiles = queries // lanes
    scale = width ** -0.5
    c2 = scale * LOG2E
    ks = slots - 2
    f32, bf16 = jnp.float32, jnp.bfloat16
    per = lanes // tile * (2 if split else 1)
    hr = lanes // per
    subs = step_rows // block
    tall = vt_scr.shape[0]

    def dot(a, b, dims=NN):
        return lax.dot_general(a, b, dims, preferred_element_type=f32)

    def prep(c, _):
        for src, base, s0 in ((own_ref, 0, ks), (oth_ref, half, oth_ref.shape[1] - 2)):
            k = src[c, s0]
            v = src[c, s0 + 1]
            at = pl.ds(pl.multiple_of((base + c) * tile, tile), tile)
            k_scr[at, :] = k
            v_scr[at, :] = v
            kt_scr[:, at] = k.T
            vt_scr[0:width, at] = v.T
            vt_scr[width:, at] = jnp.ones((tall - width, tile), bf16)
            dk_scr[at, :] = jnp.zeros((tile, width), f32)
            dv_scr[at, :] = jnp.zeros((tile, width), f32)
        return 0

    core = lax.axis_index("seq") % 2
    chip = lax.axis_index("seq") // 2
    head = half + chip // 2 if split else chip
    fetch = pltpu.make_async_copy(masks_ref.at[head], mask_scr, sem)
    fetch.start()
    lax.fori_loop(0, half, prep, 0)
    fetch.wait()
    blocks = 2 * half
    key = lax.broadcasted_iota(jnp.int32, (blocks, blocks), 0)
    from_block = lax.broadcasted_iota(jnp.int32, (blocks, blocks), 1)
    source = 2 * (key % half) + jnp.where(key < half, core, 1 - core)
    pick = (source == from_block).astype(f32).astype(bf16)
    seen = dot(pick, (mask_scr[...] > 0).astype(f32).astype(bf16), NT).astype(bf16)
    lane = lax.broadcasted_iota(jnp.int32, (blocks, lanes), 1)
    row = lax.broadcasted_iota(jnp.int32, (blocks, lanes), 0)
    for t in range(tiles):
        spread = (2 * (lane // hr + per * t) + core == row).astype(f32).astype(bf16)
        bias_ref[t] = jnp.where(dot(seen, spread) > 0.5, 0.0, -1e30)

    def q_tile(t):
        if split:
            return jnp.concatenate([own_ref[per * t + i, 0, :hr] for i in range(per)], 0)
        return jnp.concatenate([own_ref[per * t + i, 0] for i in range(per)], 0)

    def g_tile(t):
        if split:
            return jnp.concatenate([own_ref[per * t + i, 0, hr:] for i in range(per)], 0)
        return jnp.concatenate([own_ref[per * t + i, 1] for i in range(per)], 0)

    def put(t, slot, x):
        for i in range(per):
            part = x[i * hr : (i + 1) * hr].astype(bf16)
            if split:
                rows_ref[per * t + i, 0, slot * hr : (slot + 1) * hr] = part
            else:
                rows_ref[per * t + i, slot] = part

    def stage(t):
        scores, probs, grads = t + 1 < tiles, 0 <= t < tiles, 0 <= t - 1
        q_next = q_tile(t + 1) if scores else None
        if grads:
            g, (qn, gn, delta, _) = g_tile(t - 1), closed[t - 1]
        if probs:
            top = jnp.max(tops[t], axis=0, keepdims=True) * c2

        def step(i, carry):
            best, o, dq = carry
            at = pl.ds(at_multiple(i * step_rows, step_rows), step_rows)
            ds_all, p_all = [], []
            for u in range(subs):
                row = at_multiple(i * step_rows + u * block, block)
                sub = pl.ds(row, block)
                if grads:
                    pb = p_scr[sub, :]
                    dp = dot(v_scr[sub, :], g, NT)
                    ds = pb * (dp - delta).astype(bf16)
                    dv_scr[sub, :] += dot(pb, gn)
                    dk_scr[sub, :] += dot(ds, qn)
                    ds_all.append(ds)
                if probs:
                    pb = jnp.exp2(x_scr[sub, :] * c2 - top).astype(bf16)
                    p_scr[sub, :] = pb
                    p_all.append(pb)
                if scores:
                    s = dot(k_scr[sub, :], q_next, NT).reshape(block // tile, tile, lanes)
                    for w in range(block // tile):
                        x = s[w] + bias_ref[t + 1, pl.ds(i * (step_rows // tile) + u * (block // tile) + w, 1), :]
                        x_scr[pl.ds(at_multiple(row + w * tile, tile), tile), :] = x
                        best = jnp.maximum(best, jnp.max(x.reshape(tile // 8, 8, lanes), axis=0))
            if grads:
                dq = dq + dot(kt_scr[:, at], jnp.concatenate(ds_all, 0))
            if probs:
                o = o + dot(vt_scr[:, at], jnp.concatenate(p_all, 0))
            return best, o, dq

        start = (
            jnp.full((8, lanes), -1e30, f32) if scores else 0,
            jnp.zeros((tall, lanes), f32) if probs else 0,
            jnp.zeros((width, lanes), f32) if grads else 0,
        )
        best, o, dq = step(0, start) if keys == step_rows else lax.fori_loop(0, keys // step_rows, step, start)
        if scores:
            tops[t + 1] = best
        if grads:
            put(t - 1, 1, (dq * (closed[t - 1][3] * scale)).T)
        if probs:
            rl = 1.0 / o[width : width + 1]
            ot = o[:width] * rl
            put(t, 0, ot.T)
            gf = g_tile(t).astype(f32)
            delta = jnp.sum(gf.T * ot, axis=0, keepdims=True)
            column = jnp.broadcast_to(rl, (width, lanes)).T
            closed[t] = ((q_tile(t).astype(f32) * column).astype(bf16), (gf * column).astype(bf16), delta, rl)

    tops, closed = {}, {}
    for t in range(-1, tiles + 1):
        stage(t)

    def finish(c, _):
        for base, ref, slot in ((0, rows_ref, slots - 2), (half, give_ref, 0)):
            at = pl.ds(pl.multiple_of((base + c) * tile, tile), tile)
            ref[c, slot] = (dk_scr[at, :] * scale).astype(bf16)
            ref[c, slot + 1] = dv_scr[at, :].astype(bf16)
        return 0

    lax.fori_loop(0, half, finish, 0)


def attend_call(masks, own, oth, first, split):
    half, slots, tile, width = own.shape
    keys = 2 * half * tile
    rows = half * tile // (2 if split else 1)
    lanes = min(LANES, rows)
    f32, bf16 = jnp.float32, jnp.bfloat16
    vm = pl.BlockSpec(memory_space=pltpu.VMEM)
    any_ = pl.BlockSpec(memory_space=pl.ANY)
    return pl.pallas_call(
        functools.partial(dense_kernel, BLOCK, min(STEP, keys), lanes, split),
        out_shape=(
            jax.ShapeDtypeStruct((half, slots, tile, width), bf16),
            jax.ShapeDtypeStruct((half, 2, tile, width), bf16),
        ),
        in_specs=[any_, vm, vm] + [any_] * len(first),
        out_specs=[vm, vm],
        scratch_shapes=[
            pltpu.VMEM((keys, width), bf16),
            pltpu.VMEM((keys, width), bf16),
            pltpu.VMEM((width, keys), bf16),
            pltpu.VMEM((width + 16, keys), bf16),
            pltpu.VMEM((keys, width), f32),
            pltpu.VMEM((keys, width), f32),
            pltpu.VMEM((keys, lanes), f32),
            pltpu.VMEM((keys, lanes), bf16),
            pltpu.VMEM((rows // lanes, 2 * half, lanes), f32),
            pltpu.VMEM((2 * half, 2 * half), jnp.int32),
            pltpu.SemaphoreType.DMA(()),
        ],
        compiler_params=pltpu.CompilerParams(vmem_limit_bytes=36 * 2**20),
        cost_estimate=pl.CostEstimate(
            flops=12 * rows * keys * width, bytes_accessed=8 * keys * width * 2, transcendentals=rows * keys
        ),
    )(masks, own, oth, *first)


def pack_kernel(chips, width, q_ref, k_ref, v_ref, g_ref, a_ref, b_ref, held, a_scr, b_scr, in_sems, out_sems):
    rows, total = held.shape[1:]
    hr = rows // 2
    copies = [
        pltpu.make_async_copy(ref, held.at[n], in_sems.at[n]) for n, ref in enumerate((q_ref, g_ref, k_ref, v_ref))
    ]
    for copy in copies:
        copy.start()
    sends = []
    for n, copy in enumerate(copies):
        copy.wait()
        for i in range(chips):
            a_scr[i, n] = held[n, :, i * width : (i + 1) * width]
            at = slice((chips + i // 2) * width, (chips + i // 2 + 1) * width)
            if n < 2:
                b_scr[i, 0, n * hr : (n + 1) * hr] = held[n, i % 2 * hr : (i % 2 + 1) * hr, at]
            else:
                b_scr[i, n - 1] = held[n, :, at]
        sends.append(pltpu.make_async_copy(a_scr.at[:, n], a_ref.at[:, n], out_sems.at[n]))
        if n > 0:
            sends.append(pltpu.make_async_copy(b_scr.at[:, n - 1], b_ref.at[:, n - 1], out_sems.at[3 + n]))
        for send in sends[-2 if n else -1 :]:
            send.start()
    for send in sends:
        send.wait()


def pack_call(arrays, chips, width):
    rows, total = arrays[0].shape
    bf16 = jnp.bfloat16
    hbm = pl.BlockSpec(memory_space=pltpu.HBM)
    shapes = [(chips, slots, rows, width) for slots in (4, 3)]
    return pl.pallas_call(
        functools.partial(pack_kernel, chips, width),
        out_shape=[jax.ShapeDtypeStruct(shape, bf16) for shape in shapes],
        in_specs=[hbm] * 4,
        out_specs=[hbm] * 2,
        scratch_shapes=[pltpu.VMEM((4, rows, total), bf16)]
        + [pltpu.VMEM(shape, bf16) for shape in shapes]
        + [pltpu.SemaphoreType.DMA((4,)), pltpu.SemaphoreType.DMA((7,))],
        compiler_params=pltpu.CompilerParams(vmem_limit_bytes=60 * 2**20),
    )(*arrays)


def unpack_kernel(chips, width, a_ref, b_ref, out_ref, query_ref, key_ref, value_ref, held, sems):
    rows = held.shape[1]
    copies = []
    for s, ref in enumerate((out_ref, query_ref, key_ref, value_ref)):
        for i in range(chips):
            held[s, :, i * width : (i + 1) * width] = a_ref[i, s]
        for i in range(chips // 2):
            at = slice((chips + i) * width, (chips + i + 1) * width)
            if s < 2:
                cut = slice(s * (rows // 2), (s + 1) * (rows // 2))
                for part in range(2):
                    held[s, part * (rows // 2) : (part + 1) * (rows // 2), at] = b_ref[2 * i + part, 0, cut]
            else:
                one = b_ref[2 * i, s - 1].astype(jnp.float32) + b_ref[2 * i + 1, s - 1].astype(jnp.float32)
                held[s, :, at] = one.astype(jnp.bfloat16)
        copies.append(pltpu.make_async_copy(held.at[s], ref, sems.at[s]))
        copies[-1].start()
    for copy in copies:
        copy.wait()


def unpack_call(back_a, back_b, heads):
    chips, _, rows, width = back_a.shape
    vm = pl.BlockSpec(memory_space=pltpu.VMEM)
    return pl.pallas_call(
        functools.partial(unpack_kernel, chips, width),
        out_shape=[jax.ShapeDtypeStruct((rows, heads * width), jnp.bfloat16)] * 4,
        in_specs=[vm, vm],
        out_specs=[pl.BlockSpec(memory_space=pltpu.HBM)] * 4,
        scratch_shapes=[pltpu.VMEM((4, rows, heads * width), jnp.bfloat16), pltpu.SemaphoreType.DMA((4,))],
        compiler_params=pltpu.CompilerParams(vmem_limit_bytes=16 * 2**20),
    )(back_a, back_b)


def after(array, *first):
    hbm = pl.BlockSpec(memory_space=pl.ANY)
    return pl.pallas_call(
        lambda *refs: None,
        out_shape=jax.ShapeDtypeStruct(array.shape, array.dtype),
        in_specs=[hbm] * (1 + len(first)),
        out_specs=hbm,
        input_output_aliases={0: 0},
        compiler_params=pltpu.CompilerParams(vmem_limit_bytes=2**20),
    )(array, *first)


def body(query, key_in, value, grad_out, masks):
    peers = lax.axis_size("seq")
    chips = peers // 2
    heads = masks.shape[0]
    width = query.shape[1] // heads
    groups = [list(range(e, peers, 2)) for e in range(2)]
    swap = [(i, i ^ 1) for i in range(peers)]

    def exchange(array):
        return lax.all_to_all(array, "seq", 0, 0, axis_index_groups=groups, tiled=True)

    def gather(rows, give):
        taken = lax.ppermute(give, "seq", swap)
        total = rows[:, -2:].astype(jnp.float32) + taken.astype(jnp.float32)
        return rows.at[:, -2:].set(total.astype(jnp.bfloat16))

    arrays = (query, key_in, value, grad_out)
    send_a, send_b = pack_call(arrays, chips, width)
    got_a = exchange(send_a)
    got_b = exchange(send_b)
    other_a = lax.ppermute(got_a, "seq", swap)
    rows_a, give_a = attend_call(masks, got_a, other_a, (), False)
    back_a = gather(rows_a, after(give_a, got_b))
    other_b = lax.ppermute(got_b, "seq", swap)
    rows_b, give_b = attend_call(masks, got_b, other_b, (back_a,), True)
    back_a = exchange(back_a)
    back_b = exchange(gather(rows_b, after(give_b, back_a)))
    return tuple(unpack_call(back_a, back_b, heads))


def solution(mesh):
    tokens = P(("dp", "seq"), None)
    return jax.shard_map(
        body,
        mesh=mesh,
        in_specs=(tokens, tokens, tokens, tokens, P("dp", None, None)),
        out_specs=(tokens, tokens, tokens, tokens),
        check_vma=False,
    )
```

profile of v0, /device:TPU:0, one launch (start us, length us, event | category | flops | bytes accessed | tf_op | source)
XLA Modules:
  0.0 158.1 jit_solution(1073050220859502551)
XLA Ops:
  0.6 3.2 %shard_map.84 = (bf16[16,4,128,128]{3,2,1,0:T(8,128)(2,1)}, bf16[16,3,128,128]{3,2,1,0:T(8,128)(2,1)}) custom-call(bf16[128,3072]{1,0:T(8,128)(2,1)} %q_ref.1, bf16[128,3072]{1,0:T(8,128)(2,1)} %k_ref.1, bf16[128,3072]{1,0:T(8,128)(2,1)} %v_ref.1, bf16[128,3072]{1,0:T(8,128)(2,1)} %g_ref.1), custom_call_target="tpu_custom_call" | custom-call | tf_op jit(solution)/shard_map/pallas_call | solution.py:231
  3.9 36.4 %all_to_all.20.own_ref = bf16[16,4,128,128]{3,2,1,0:T(8,128)(2,1)S(1)} all-to-all(bf16[16,4,128,128]{3,2,1,0:T(8,128)(2,1)} %get-tuple-element.34), channel_id=1, replica_groups={{0,2,4,6,8,10,12,14,16,18,20,22,24,26,28,30},{1,3,5,7,9,11,13,15,17,19,..., dimensions={0} | all-to-all | bytes 4194304 | tf_op jit(solution)/shard_map/all_to_all | solution.py:298
  40.2 0.0 copy-start.2
  40.2 0.0 collective-permute-start
  40.2 4.5 %all-to-all-start.1 = ((bf16[16,3,128,128]{3,2,1,0:T(8,128)(2,1)}), bf16[16,3,128,128]{3,2,1,0:T(8,128)(2,1)}, u32[]{:S(2)}, u32[]{:S(2)}) async-start(bf16[16,3,128,128]{3,2,1,0:T(8,128)(2,1)} %get-tuple-element.37), calls=%async_computation.1 | async-start | bytes 3145728 | tf_op jit(solution)/shard_map/all_to_all | solution.py:298
  44.8 0.0 collective-permute-done.oth_ref
  44.8 0.0 copy-done.2
  44.8 35.6 %shard_map.85 = (bf16[16,4,128,128]{3,2,1,0:T(8,128)(2,1)}, bf16[16,2,128,128]{3,2,1,0:T(8,128)(2,1)S(1)}) custom-call(s32[24,32,32]{2,1,0:T(8,128)S(1)} %copy-done.2, bf16[16,4,128,128]{3,2,1,0:T(8,128)(2,1)S(1)} %all_to_all.20.own_ref, bf16[16,4,128,128]{3,2,1,0:T(8,128)(2,1)} %collective-permute-done.oth_ref), custom_call_target="tpu_custom_call" | custom-call | flops 12884901888 | bytes 8388608 | tf_op jit(solution)/shard_map/pallas_call | solution.py:171
  80.4 0.0 all-to-all-done.1.refs_1_.own_ref
  80.5 0.5 collective-permute-start.1
  80.9 0.1 collective-permute-start.2
  81.0 2.3 %collective-permute-done.1 = bf16[16,2,128,128]{3,2,1,0:T(8,128)(2,1)S(1)} collective-permute-done((bf16[16,2,128,128]{3,2,1,0:T(8,128)(2,1)S(1)}, bf16[16,2,128,128]{3,2,1,0:T(8,128)(2,1)S(1)}, u32[]{:S(2)}, u32[]{:S(2)}) %collective-permute-start.1) | collective-permute-done | bytes 1048608 | tf_op jit(solution)/shard_map/ppermute | solution.py:301
  83.3 2.6 %fusion.refs_0_ = bf16[16,4,128,128]{3,2,1,0:T(8,128)(2,1)} fusion(bf16[16,4,128,128]{3,2,1,0:T(8,128)(2,1)} %get-tuple-element.35, bf16[16,2,128,128]{3,2,1,0:T(8,128)(2,1)S(1)} %collective-permute-done.1), kind=kLoop, calls=%fused_computation.2 | loop fusion | flops 2097152 | bytes 3145728 | tf_op jit(solution)/shard_map/scatter | solution.py:303
  85.9 7.5 %all-to-all-start.2 = ((bf16[16,4,128,128]{3,2,1,0:T(8,128)(2,1)}), bf16[16,4,128,128]{3,2,1,0:T(8,128)(2,1)S(1)}, u32[]{:S(2)}, u32[]{:S(2)}) async-start(bf16[16,4,128,128]{3,2,1,0:T(8,128)(2,1)} %fusion.refs_0_), calls=%async_computation.2 | async-start | bytes 4194304 | tf_op jit(solution)/shard_map/all_to_all | solution.py:298
  93.5 0.0 collective-permute-done.2.oth_ref
  93.5 19.7 %shard_map.87 = (bf16[16,3,128,128]{3,2,1,0:T(8,128)(2,1)S(1)}, bf16[16,2,128,128]{3,2,1,0:T(8,128)(2,1)S(1)}) custom-call(s32[24,32,32]{2,1,0:T(8,128)S(1)} %copy-done.2, bf16[16,3,128,128]{3,2,1,0:T(8,128)(2,1)} %all-to-all-done.1.refs_1_.own_ref, bf16[16,3,128,128]{3,2,1,0:T(8,128)(2,1)} %collective-permute-done.2.oth_ref, ...), custom_call_target="tpu_custom_call" | custom-call | flops 6442450944 | bytes 8388608 | tf_op jit(solution)/shard_map/pallas_call | solution.py:171
  113.2 0.0 copy-start
  113.2 1.2 copy-done
  114.3 12.0 %all-to-all-done.2.refs_1_.a_ref = bf16[16,4,128,128]{3,2,1,0:T(8,128)(2,1)S(1)} async-done(((bf16[16,4,128,128]{3,2,1,0:T(8,128)(2,1)}), bf16[16,4,128,128]{3,2,1,0:T(8,128)(2,1)S(1)}, u32[]{:S(2)}, u32[]{:S(2)}) %all-to-all-start.2) | async-done | bytes 2097184 | tf_op jit(solution)/shard_map/all_to_all | solution.py:298
  126.3 0.0 copy-start.1
  126.3 0.0 collective-permute-start.3
  126.3 2.7 %collective-permute-done.3 = bf16[16,2,128,128]{3,2,1,0:T(8,128)(2,1)S(1)} collective-permute-done((bf16[16,2,128,128]{3,2,1,0:T(8,128)(2,1)S(1)}, bf16[16,2,128,128]{3,2,1,0:T(8,128)(2,1)S(1)}, u32[]{:S(2)}, u32[]{:S(2)}) %collective-permute-start.3) | collective-permute-done | bytes 1048608 | tf_op jit(solution)/shard_map/ppermute | solution.py:301
  129.0 0.0 copy-done.1
  129.0 0.5 fusion.1
  129.5 26.5 %all_to_all.21.b_ref = bf16[16,3,128,128]{3,2,1,0:T(8,128)(2,1)S(1)} all-to-all(bf16[16,3,128,128]{3,2,1,0:T(8,128)(2,1)S(1)} %fusion.1), channel_id=1, replica_groups={{0,2,4,6,8,10,12,14,16,18,20,22,24,26,28,30},{1,3,5,7,9,11,13,15,17,19,..., dimensions={0} | all-to-all | bytes 3145728 | tf_op jit(solution)/shard_map/all_to_all | solution.py:298
  156.1 1.9 %shard_map.89 = (bf16[128,3072]{1,0:T(8,128)(2,1)}, bf16[128,3072]{1,0:T(8,128)(2,1)}, bf16[128,3072]{1,0:T(8,128)(2,1)}, bf16[128,3072]{1,0:T(8,128)(2,1)}) custom-call(bf16[16,4,128,128]{3,2,1,0:T(8,128)(2,1)S(1)} %all-to-all-done.2.refs_1_.a_ref, bf16[16,3,128,128]{3,2,1,0:T(8,128)(2,1)S(1)} %all_to_all.21.b_ref), custom_call_target="tpu_custom_call" | custom-call | tf_op jit(solution)/shard_map/pallas_call | solution.py:267
  (2 shorter events, 0.0 us)
Async XLA Ops:
  40.2 4.6 %copy-start.2 = (s32[24,32,32]{2,1,0:T(8,128)S(1)}, s32[24,32,32]{2,1,0:T(8,128)}, u32[]{:S(2)}) copy-start(s32[24,32,32]{2,1,0:T(8,128)} %masks_ref.3) | copy-start | bytes 294916
  40.2 4.5 %collective-permute-start = (bf16[16,4,128,128]{3,2,1,0:T(8,128)(2,1)S(1)}, bf16[16,4,128,128]{3,2,1,0:T(8,128)(2,1)}, u32[]{:S(2)}, u32[]{:S(2)}) collective-permute-start(bf16[16,4,128,128]{3,2,1,0:T(8,128)(2,1)S(1)} %all_to_all.20.own_ref), channel_id=1, source_target_pairs={{0,1},{1,0},{2,3},{3,2},{4,5},{5,4},{6,7},{7,6},{8,9},{9,8},{10,11... | collective-permute-start | bytes 6291464 | tf_op jit(solution)/shard_map/ppermute | solution.py:309
  40.2 40.2 %all-to-all-start.1 = ((bf16[16,3,128,128]{3,2,1,0:T(8,128)(2,1)}), bf16[16,3,128,128]{3,2,1,0:T(8,128)(2,1)}, u32[]{:S(2)}, u32[]{:S(2)}) async-start(bf16[16,3,128,128]{3,2,1,0:T(8,128)(2,1)} %get-tuple-element.37), calls=%async_computation.1 | async-start | bytes 3145728 | tf_op jit(solution)/shard_map/all_to_all | solution.py:298
  80.5 2.9 %collective-permute-start.1 = (bf16[16,2,128,128]{3,2,1,0:T(8,128)(2,1)S(1)}, bf16[16,2,128,128]{3,2,1,0:T(8,128)(2,1)S(1)}, u32[]{:S(2)}, u32[]{:S(2)}) collective-permute-start(bf16[16,2,128,128]{3,2,1,0:T(8,128)(2,1)S(1)} %shard_map.86), channel_id=1, source_target_pairs={{0,1},{1,0},{2,3},{3,2},{4,5},{5,4},{6,7},{7,6},{8,9},{9,8},{10,11... | collective-permute-start | bytes 3145736 | tf_op jit(solution)/shard_map/ppermute | solution.py:301
  80.9 12.6 %collective-permute-start.2 = (bf16[16,3,128,128]{3,2,1,0:T(8,128)(2,1)}, bf16[16,3,128,128]{3,2,1,0:T(8,128)(2,1)}, u32[]{:S(2)}, u32[]{:S(2)}) collective-permute-start(bf16[16,3,128,128]{3,2,1,0:T(8,128)(2,1)} %all-to-all-done.1.refs_1_.own_ref), channel_id=1, source_target_pairs={{0,1},{1,0},{2,3},{3,2},{4,5},{5,4},{6,7},{7,6},{8,9},{9,8},{10,11... | collective-permute-start | bytes 4718600 | tf_op jit(solution)/shard_map/ppermute | solution.py:312
  85.9 40.4 %all-to-all-start.2 = ((bf16[16,4,128,128]{3,2,1,0:T(8,128)(2,1)}), bf16[16,4,128,128]{3,2,1,0:T(8,128)(2,1)S(1)}, u32[]{:S(2)}, u32[]{:S(2)}) async-start(bf16[16,4,128,128]{3,2,1,0:T(8,128)(2,1)} %fusion.refs_0_), calls=%async_computation.2 | async-start | bytes 4194304 | tf_op jit(solution)/shard_map/all_to_all | solution.py:298
  113.2 1.2 copy-start
  126.3 2.7 %copy-start.1 = (bf16[16,3,128,128]{3,2,1,0:T(8,128)(2,1)S(1)}, bf16[16,3,128,128]{3,2,1,0:T(8,128)(2,1)}, u32[]{:S(2)}) copy-start(bf16[16,3,128,128]{3,2,1,0:T(8,128)(2,1)} %copy-done) | copy-start | bytes 4718596
  126.3 2.7 %collective-permute-start.3 = (bf16[16,2,128,128]{3,2,1,0:T(8,128)(2,1)S(1)}, bf16[16,2,128,128]{3,2,1,0:T(8,128)(2,1)S(1)}, u32[]{:S(2)}, u32[]{:S(2)}) collective-permute-start(bf16[16,2,128,128]{3,2,1,0:T(8,128)(2,1)S(1)} %shard_map.88), channel_id=1, source_target_pairs={{0,1},{1,0},{2,3},{3,2},{4,5},{5,4},{6,7},{7,6},{8,9},{9,8},{10,11... | collective-permute-start | bytes 3145736 | tf_op jit(solution)/shard_map/ppermute | solution.py:301
where the time goes:
time: 159 us; the launch traced here: 158 us
  blocking collectives  62.9 us (40%)
  Pallas kernels  60.4 us (38%)
  waiting for transfers between devices  17 us (11%)
  starting transfers between devices  12.7 us (8%)
  other arithmetic  3.08 us (2%)
    all_to_all x2, blocking collectives, exchange(): lax.all_to_all(array, 'seq', 0, 0, axis_index_groups=groups, tiled=True)  62.9 us
    pallas_call x2, Pallas kernels, attend_call(): pl.pallas_call(functools.partial(dense_kernel, BLOCK, min(STEP, keys), la...  55.3 us
    all_to_all x2, starting transfers between devices, exchange(): lax.all_to_all(array, 'seq', 0, 0, axis_index_groups=groups, tiled=True)  12.1 us
    all_to_all x2, waiting for transfers between devices, exchange(): lax.all_to_all(array, 'seq', 0, 0, axis_index_groups=groups, tiled=True)  12 us
    ppermute x2, waiting for transfers between devices, gather(): taken = lax.ppermute(give, 'seq', swap)  4.96 us
    pallas_call x1, Pallas kernels, pack_call(): pl.pallas_call(functools.partial(pack_kernel, chips, width), out_shape=[j...  3.24 us
  transfers between devices with their start and end apart: 6, of which 3 were waited for; matrix products, arithmetic and copies ran while one was open for 2% of the time, Pallas kernels for 35%

commit v1 on v0

v1 whole, which is shorter than its diff:
```python
import functools

import jax
import jax.numpy as jnp
from jax import lax
from jax.experimental import pallas as pl
from jax.experimental.pallas import tpu as pltpu
from jax.sharding import PartitionSpec as P

LANES = 512
BLOCK = 512
STEPS_WHOLE = (4096, 4096, 4096, 4096, 4096)
STEPS_SPLIT = (512, 512, 512, 512, 512)
NT = (((1,), (1,)), ((), ()))
NN = (((1,), (0,)), ((), ()))
LOG2E = 1.4426950408889634


def at_multiple(x, n):
    return x if isinstance(x, int) else pl.multiple_of(x, n)


def attend_kernel(
    steps, lanes, split, depends, masks_ref, own_ref, oth_ref, *refs
):
    send_ref, keep_ref, give_ref = refs[depends : depends + 3]
    (rows_scr, qg_scr, k_scr, v_scr, kt_scr, vt_scr, dk_scr, dv_scr, x_scr, p_scr, bias_scr, mask_scr) = refs[depends + 3 : depends + 15]
    (top_scr, qn_scr, gn_scr, stat_scr, give_scr, keep_scr, sems) = refs[depends + 15 :]
    half, slots, tile, width = own_ref.shape
    blocks = 2 * half
    keys = blocks * tile
    queries = half * tile // (2 if split else 1)
    tiles = queries // lanes
    scale = width ** -0.5
    c2 = scale * LOG2E
    ks = slots - 2
    f32, bf16 = jnp.float32, jnp.bfloat16
    per = lanes // tile * (2 if split else 1)
    hr = lanes // per
    tall = vt_scr.shape[0]

    def dot(a, b, dims=NN):
        return lax.dot_general(a, b, dims, preferred_element_type=f32)

    core = lax.axis_index("seq") % 2
    chip = lax.axis_index("seq") // 2
    head = half + chip // 2 if split else chip
    copies = [
        pltpu.make_async_copy(masks_ref.at[head], mask_scr, sems.at[0]),
        pltpu.make_async_copy(own_ref.at[:, ks], k_scr.at[0:half], sems.at[1]),
        pltpu.make_async_copy(oth_ref.at[:, ks], k_scr.at[half:blocks], sems.at[2]),
        pltpu.make_async_copy(own_ref.at[:, 0:ks], qg_scr, sems.at[3]),
        pltpu.make_async_copy(own_ref.at[:, ks + 1], v_scr.at[0:half], sems.at[4]),
        pltpu.make_async_copy(oth_ref.at[:, ks + 1], v_scr.at[half:blocks], sems.at[5]),
    ]
    for copy in copies:
        copy.start()
    copies[0].wait()

    key = lax.broadcasted_iota(jnp.int32, (blocks, blocks), 0)
    from_block = lax.broadcasted_iota(jnp.int32, (blocks, blocks), 1)
    source = 2 * (key % half) + jnp.where(key < half, core, 1 - core)
    pick = (source == from_block).astype(f32).astype(bf16)
    seen = dot(pick, (mask_scr[...] > 0).astype(f32).astype(bf16), NT).astype(bf16)
    lane = lax.broadcasted_iota(jnp.int32, (blocks, lanes), 1)
    row = lax.broadcasted_iota(jnp.int32, (blocks, lanes), 0)
    for t in range(tiles):
        spread = (2 * (lane // hr + per * t) + core == row).astype(f32).astype(bf16)
        bias_scr[t] = jnp.where(dot(seen, spread) > 0.5, 0.0, -1e30)
    for copy in copies[1:]:
        copy.wait()

    def q_tile(t):
        if split:
            return jnp.concatenate([qg_scr[per * t + i, 0, :hr] for i in range(per)], 0)
        return jnp.concatenate([qg_scr[per * t + i, 0] for i in range(per)], 0)

    def g_tile(t):
        if split:
            return jnp.concatenate([qg_scr[per * t + i, 0, hr:] for i in range(per)], 0)
        return jnp.concatenate([qg_scr[per * t + i, 1] for i in range(per)], 0)

    def put(t, slot, x):
        for i in range(per):
            part = x[i * hr : (i + 1) * hr].astype(bf16)
            if split:
                rows_scr[per * t + i, 0, slot * hr : (slot + 1) * hr] = part
            else:
                rows_scr[per * t + i, slot] = part

    def stage(t, scores, probs, grads, step_rows):
        prepare = not probs and not grads
        subs = step_rows // BLOCK
        if scores:
            q_next = q_tile(t + 1)
        if grads:
            g, qn, gn = g_tile(t - 1), qn_scr[...], gn_scr[...]
            delta, rl_last = stat_scr[0:1, :], stat_scr[1:2, :]
        if probs:
            top = jnp.max(top_scr[...], axis=0, keepdims=True) * c2

        def step(i, carry):
            best, o, dq = carry
            at = pl.ds(at_multiple(i * step_rows, step_rows), step_rows)
            ds_all, p_all = [], []
            for u in range(subs):
                first = i * step_rows + u * BLOCK
                sub = pl.ds(at_multiple(first, BLOCK), BLOCK)
                pair = pl.ds(i * (step_rows // tile) + u * (BLOCK // tile), BLOCK // tile)
                if grads:
                    pb = p_scr[sub, :]
                    dp = dot(v_scr[pair].reshape(BLOCK, width), g, NT)
                    ds = pb * (dp - delta).astype(bf16)
                    dv_scr[sub, :] += dot(pb, gn)
                    dk_scr[sub, :] += dot(ds, qn)
                    ds_all.append(ds)
                if probs:
                    pb = jnp.exp2(x_scr[sub, :] * c2 - top).astype(bf16)
                    p_scr[sub, :] = pb
                    p_all.append(pb)
                if scores:
                    s = dot(k_scr[pair].reshape(BLOCK, width), q_next, NT).reshape(BLOCK // tile, tile, lanes)
                    for w in range(BLOCK // tile):
                        x = s[w] + bias_scr[t + 1, pl.ds(i * (step_rows // tile) + u * (BLOCK // tile) + w, 1), :]
                        x_scr[pl.ds(at_multiple(first + w * tile, tile), tile), :] = x
                        best = jnp.maximum(best, jnp.max(x.reshape(tile // 8, 8, lanes), axis=0))
                if prepare:
                    for w in range(BLOCK // tile):
                        j = i * (step_rows // tile) + u * (BLOCK // tile) + w
                        to = pl.ds(at_multiple(first + w * tile, tile), tile)
                        kt_scr[:, to] = k_scr[j].T
                        vt_scr[0:width, to] = v_scr[j].T
                        vt_scr[width:, to] = jnp.ones((tall - width, tile), bf16)
                        dk_scr[to, :] = jnp.zeros((tile, width), f32)
                        dv_scr[to, :] = jnp.zeros((tile, width), f32)
            if grads:
                dq = dq + dot(kt_scr[:, at], jnp.concatenate(ds_all, 0))
            if probs:
                o = o + dot(vt_scr[:, at], jnp.concatenate(p_all, 0))
            return best, o, dq

        start = (
            jnp.full((8, lanes), -1e30, f32) if scores else 0,
            jnp.zeros((tall, lanes), f32) if probs else 0,
            jnp.zeros((width, lanes), f32) if grads else 0,
        )
        if keys == step_rows:
            best, o, dq = step(0, start)
        else:
            best, o, dq = lax.fori_loop(0, keys // step_rows, step, start)
        if scores:
            top_scr[...] = best
        if grads:
            put(t - 1, 1, (dq * (rl_last * scale)).T)
        if probs:
            rl = 1.0 / o[width : width + 1]
            ot = o[:width] * rl
            put(t, 0, ot.T)
            gf = g_tile(t).astype(f32)
            stat_scr[0:1, :] = jnp.sum(gf.T * ot, axis=0, keepdims=True)
            stat_scr[1:2, :] = rl
            column = jnp.broadcast_to(rl, (width, lanes)).T
            qn_scr[...] = (q_tile(t).astype(f32) * column).astype(bf16)
            gn_scr[...] = (gf * column).astype(bf16)

    stage(-1, True, False, False, steps[0])
    stage(0, True, True, False, steps[1])

    if tiles > 2:

        def middle(t, _):
            stage(t, True, True, True, steps[2])
            return 0

        lax.fori_loop(1, tiles - 1, middle, 0)
    stage(tiles - 1, False, True, True, steps[3])
    stage(tiles, False, False, True, steps[4])
    rows_out = pltpu.make_async_copy(rows_scr, send_ref.at[:, 0:ks], sems.at[0])
    rows_out.start()

    def finish(base, ref):
        def copy(c, _):
            at = pl.ds(pl.multiple_of((base + c) * tile, tile), tile)
            ref[c, 0] = (dk_scr[at, :] * scale).astype(bf16)
            ref[c, 1] = dv_scr[at, :].astype(bf16)
            return 0

        lax.fori_loop(0, half, copy, 0)

    finish(half, give_scr)
    give_out = pltpu.make_async_copy(give_scr, give_ref, sems.at[1])
    give_out.start()
    finish(0, keep_scr)
    keep_out = pltpu.make_async_copy(keep_scr, keep_ref, sems.at[2])
    keep_out.start()
    rows_out.wait()
    give_out.wait()
    keep_out.wait()


def attend_call(masks, own, oth, depends, split):
    half, slots, tile, width = own.shape
    keys = 2 * half * tile
    rows = half * tile // (2 if split else 1)
    lanes = min(LANES, rows // 2)
    f32, bf16 = jnp.float32, jnp.bfloat16
    any_ = pl.BlockSpec(memory_space=pl.ANY)
    hbm = pl.BlockSpec(memory_space=pltpu.HBM)
    return pl.pallas_call(
        functools.partial(attend_kernel, STEPS_SPLIT if split else STEPS_WHOLE, lanes, split, len(depends)),
        out_shape=(
            jax.ShapeDtypeStruct((half, slots, tile, width), bf16),
            jax.ShapeDtypeStruct((half, 2, tile, width), bf16),
            jax.ShapeDtypeStruct((half, 2, tile, width), bf16),
        ),
        in_specs=[any_] * (3 + len(depends)),
        out_specs=[hbm, hbm, hbm],
        scratch_shapes=[
            pltpu.VMEM((half, slots - 2, tile, width), bf16),
            pltpu.VMEM((half, slots - 2, tile, width), bf16),
            pltpu.VMEM((2 * half, tile, width), bf16),
            pltpu.VMEM((2 * half, tile, width), bf16),
            pltpu.VMEM((width, keys), bf16),
            pltpu.VMEM((width + 16, keys), bf16),
            pltpu.VMEM((keys, width), f32),
            pltpu.VMEM((keys, width), f32),
            pltpu.VMEM((keys, lanes), f32),
            pltpu.VMEM((keys, lanes), bf16),
            pltpu.VMEM((rows // lanes, 2 * half, lanes), f32),
            pltpu.VMEM((2 * half, 2 * half), jnp.int32),
            pltpu.VMEM((8, lanes), f32),
            pltpu.VMEM((lanes, width), bf16),
            pltpu.VMEM((lanes, width), bf16),
            pltpu.VMEM((8, lanes), f32),
            pltpu.VMEM((half, 2, tile, width), bf16),
            pltpu.VMEM((half, 2, tile, width), bf16),
            pltpu.SemaphoreType.DMA((6,)),
        ],
        compiler_params=pltpu.CompilerParams(vmem_limit_bytes=(251 if split else 248) * 2**18),
        cost_estimate=pl.CostEstimate(
            flops=12 * rows * keys * width, bytes_accessed=8 * keys * width * 2, transcendentals=rows * keys
        ),
    )(masks, own, oth, *depends)


def join_kernel(rows_ref, keep_ref, taken_ref, *refs):
    send_ref, keep_scr, taken_scr, sum_scr, sems = refs[-5:]
    chips, slots = send_ref.shape[:2]
    parts = sems.shape[1]
    cuts = [pl.ds(n * (chips // parts), chips // parts) for n in range(parts)]
    loads = [
        pltpu.make_async_copy(ref.at[cut], scr.at[cut], sems.at[k, n])
        for n, cut in enumerate(cuts)
        for k, (ref, scr) in enumerate(((keep_ref, keep_scr), (taken_ref, taken_scr)))
    ]
    stores = [
        pltpu.make_async_copy(sum_scr.at[cut], send_ref.at[cut, slots - 2 : slots], sems.at[2, n])
        for n, cut in enumerate(cuts)
    ]
    for load in loads:
        load.start()
    for n in range(parts):
        loads[2 * n].wait()
        loads[2 * n + 1].wait()

        def add(c, _):
            for s in range(2):
                total = keep_scr[c, s].astype(jnp.float32) + taken_scr[c, s].astype(jnp.float32)
                sum_scr[c, s] = total.astype(jnp.bfloat16)
            return 0

        lax.fori_loop(n * (chips // parts), (n + 1) * (chips // parts), add, 0)
        stores[n].start()
    for store in stores:
        store.wait()


def join_call(rows, keep, taken, depends, grant):
    hbm = pl.BlockSpec(memory_space=pltpu.HBM)
    return pl.pallas_call(
        join_kernel,
        out_shape=jax.ShapeDtypeStruct(rows.shape, rows.dtype),
        in_specs=[hbm] + [pl.BlockSpec(memory_space=pl.ANY)] * (2 + len(depends)),
        out_specs=hbm,
        scratch_shapes=[pltpu.VMEM(keep.shape, keep.dtype)] * 3 + [pltpu.SemaphoreType.DMA((3, 4))],
        input_output_aliases={0: 0},
        compiler_params=pltpu.CompilerParams(vmem_limit_bytes=grant),
    )(rows, keep, taken, *depends)


def pack_kernel(chips, width, q_ref, k_ref, v_ref, g_ref, a_ref, b_ref, held, a_scr, b_scr, in_sems, out_sems):
    rows, total = held.shape[1:]
    hr = rows // 2
    copies = [
        pltpu.make_async_copy(ref, held.at[n], in_sems.at[n]) for n, ref in enumerate((q_ref, g_ref, k_ref, v_ref))
    ]
    for copy in copies:
        copy.start()
    sends = []
    for n, copy in enumerate(copies):
        copy.wait()
        for i in range(chips):
            a_scr[i, n] = held[n, :, i * width : (i + 1) * width]
            at = slice((chips + i // 2) * width, (chips + i // 2 + 1) * width)
            if n < 2:
                b_scr[i, 0, n * hr : (n + 1) * hr] = held[n, i % 2 * hr : (i % 2 + 1) * hr, at]
            else:
                b_scr[i, n - 1] = held[n, :, at]
        sends.append(pltpu.make_async_copy(a_scr.at[:, n], a_ref.at[:, n], out_sems.at[n]))
        if n > 0:
            sends.append(pltpu.make_async_copy(b_scr.at[:, n - 1], b_ref.at[:, n - 1], out_sems.at[3 + n]))
        for send in sends[-2 if n else -1 :]:
            send.start()
    for send in sends:
        send.wait()


def pack_call(arrays, chips, width):
    rows, total = arrays[0].shape
    bf16 = jnp.bfloat16
    hbm = pl.BlockSpec(memory_space=pltpu.HBM)
    shapes = [(chips, slots, rows, width) for slots in (4, 3)]
    return pl.pallas_call(
        functools.partial(pack_kernel, chips, width),
        out_shape=[jax.ShapeDtypeStruct(shape, bf16) for shape in shapes],
        in_specs=[hbm] * 4,
        out_specs=[hbm] * 2,
        scratch_shapes=[pltpu.VMEM((4, rows, total), bf16)]
        + [pltpu.VMEM(shape, bf16) for shape in shapes]
        + [pltpu.SemaphoreType.DMA((4,)), pltpu.SemaphoreType.DMA((7,))],
        compiler_params=pltpu.CompilerParams(vmem_limit_bytes=248 * 2**18),
    )(*arrays)


def unpack_whole(width, a_ref, out_ref, query_ref, key_ref, value_ref, got, held, in_sems, out_sems):
    chips = got.shape[1]
    loads = [pltpu.make_async_copy(a_ref.at[:, s], got.at[s], in_sems.at[s]) for s in range(4)]
    for load in loads:
        load.start()
    stores = []
    for s, ref in enumerate((out_ref, query_ref, key_ref, value_ref)):
        loads[s].wait()
        for i in range(chips):
            held[s, :, i * width : (i + 1) * width] = got[s, i]
        stores.append(pltpu.make_async_copy(held.at[s], ref.at[:, 0 : chips * width], out_sems.at[s]))
        stores[s].start()
    for store in stores:
        store.wait()


def unpack_split(width, b_ref, *refs):
    outs, (held, sems) = refs[4:8], refs[8:]
    chips, _, rows, _ = b_ref.shape
    hr = rows // 2
    stores = []
    for s, ref in enumerate(outs):
        for i in range(chips // 2):
            at = slice(i * width, (i + 1) * width)
            if s < 2:
                for part in range(2):
                    held[s, part * hr : (part + 1) * hr, at] = b_ref[2 * i + part, 0, s * hr : (s + 1) * hr]
            else:
                one = b_ref[2 * i, s - 1].astype(jnp.float32) + b_ref[2 * i + 1, s - 1].astype(jnp.float32)
                held[s, :, at] = one.astype(jnp.bfloat16)
        to = ref.at[:, chips * width : chips * width + held.shape[2]]
        stores.append(pltpu.make_async_copy(held.at[s], to, sems.at[s]))
        stores[s].start()
    for store in stores:
        store.wait()


def unpack_call(back_a, back_b, heads):
    chips, _, rows, width = back_a.shape
    bf16 = jnp.bfloat16
    hbm = pl.BlockSpec(memory_space=pltpu.HBM)
    any_ = pl.BlockSpec(memory_space=pl.ANY)
    shapes = [jax.ShapeDtypeStruct((rows, heads * width), bf16)] * 4
    sems = [pltpu.SemaphoreType.DMA((4,)), pltpu.SemaphoreType.DMA((4,))]
    params = pltpu.CompilerParams(vmem_limit_bytes=16 * 2**20)
    whole = pl.pallas_call(
        functools.partial(unpack_whole, width),
        out_shape=shapes,
        in_specs=[any_],
        out_specs=[hbm] * 4,
        scratch_shapes=[pltpu.VMEM((4, chips, rows, width), bf16), pltpu.VMEM((4, rows, chips * width), bf16)] + sems,
        compiler_params=params,
    )(back_a)
    return pl.pallas_call(
        functools.partial(unpack_split, width),
        out_shape=shapes,
        in_specs=[pl.BlockSpec(memory_space=pltpu.VMEM)] + [hbm] * 4,
        out_specs=[hbm] * 4,
        scratch_shapes=[pltpu.VMEM((4, rows, (heads - chips) * width), bf16), pltpu.SemaphoreType.DMA((4,))],
        input_output_aliases={1: 0, 2: 1, 3: 2, 4: 3},
        compiler_params=params,
    )(back_b, *whole)


def after(array, *first):
    hbm = pl.BlockSpec(memory_space=pl.ANY)
    return pl.pallas_call(
        lambda *refs: None,
        out_shape=jax.ShapeDtypeStruct(array.shape, array.dtype),
        in_specs=[hbm] * (1 + len(first)),
        out_specs=hbm,
        input_output_aliases={0: 0},
        compiler_params=pltpu.CompilerParams(vmem_limit_bytes=248 * 2**18),
    )(array, *first)


def body(query, key_in, value, grad_out, masks):
    peers = lax.axis_size("seq")
    chips = peers // 2
    heads = masks.shape[0]
    width = query.shape[1] // heads
    groups = [list(range(e, peers, 2)) for e in range(2)]
    swap = [(i, i ^ 1) for i in range(peers)]

    def exchange(array):
        return lax.all_to_all(array, "seq", 0, 0, axis_index_groups=groups, tiled=True)

    def gather(parts, first, grant):
        rows, keep, give = parts
        return join_call(rows, keep, lax.ppermute(give, "seq", swap), (first,), grant)

    arrays = (query, key_in, value, grad_out)
    send_a, send_b = pack_call(arrays, chips, width)
    got_a = exchange(send_a)
    got_b = exchange(send_b)
    other_a = lax.ppermute(got_a, "seq", swap)
    send_a = gather(attend_call(masks, got_a, other_a, (), False), got_b, 62 * 2**20)
    got_b = after(got_b, send_a)
    other_b = lax.ppermute(got_b, "seq", swap)
    parts_b = attend_call(masks, got_b, other_b, (), True)
    back_a = exchange(send_a)
    back_b = exchange(gather(parts_b, back_a, 56 * 2**20))
    return tuple(unpack_call(back_a, back_b, heads))


def solution(mesh):
    tokens = P(("dp", "seq"), None)
    return jax.shard_map(
        body,
        mesh=mesh,
        in_specs=(tokens, tokens, tokens, tokens, P("dp", None, None)),
        out_specs=(tokens, tokens, tokens, tokens),
        check_vma=False,
    )
```

time: 159 us -> 153 us (0.962)
  blocking collectives: 62.9 us -> 36.5 us
  waiting for transfers between devices: 17 us -> 36.3 us
  Pallas kernels: 60.4 us -> 63.7 us
  other arithmetic: 3.08 us -> 0 us
  starting transfers between devices: 12.7 us -> 14.5 us
    all_to_all x2 -> x1, blocking collectives: 62.9 us -> 36.5 us  [exchange(): lax.all_to_all(array, 'seq', 0, 0, axis_index_groups=groups, tiled=True)]
    all_to_all x2 -> x3, waiting for transfers between devices: 12 us -> 32.7 us  [exchange(): lax.all_to_all(array, 'seq', 0, 0, axis_index_groups=groups, tiled=True)]
    pallas_call x3 -> x6, Pallas kernels: 57.2 us -> 60.5 us  [the longest x2 52.1 us: attend_call(): pl.pallas_call(functools.partial(attend_kernel, STEPS_SPLIT if split else...]
    scatter x2 -> x0, other arithmetic: 3.08 us -> none  [gather(): return rows.at[:, -2:].set(total.astype(jnp.bfloat16))]
    ppermute x2, waiting for transfers between devices: 4.96 us -> 2.87 us  [gather(): lax.ppermute(give, 'seq', swap)]
    all_to_all x2 -> x3, starting transfers between devices: 12.1 us -> 14 us  [exchange(): lax.all_to_all(array, 'seq', 0, 0, axis_index_groups=groups, tiled=True)]
  transfers between devices with their start and end apart: 6 -> 7, of which waited for: 3 -> 4; matrix products, arithmetic and copies ran while one was open for 2% -> 0% of each run, Pallas kernels for 35% -> 36%
where the time goes in v1:
time: 153 us
  Pallas kernels  63.7 us (42%)
  blocking collectives  36.5 us (24%)
  waiting for transfers between devices  36.3 us (24%)
  starting transfers between devices  14.5 us (9%)
    pallas_call x2, Pallas kernels, attend_call(): pl.pallas_call(functools.partial(attend_kernel, STEPS_SPLIT if split else...  52.1 us
    all_to_all x1, blocking collectives, exchange(): lax.all_to_all(array, 'seq', 0, 0, axis_index_groups=groups, tiled=True)  36.5 us
    all_to_all x3, waiting for transfers between devices, exchange(): lax.all_to_all(array, 'seq', 0, 0, axis_index_groups=groups, tiled=True)  32.7 us
    all_to_all x3, starting transfers between devices, exchange(): lax.all_to_all(array, 'seq', 0, 0, axis_index_groups=groups, tiled=True)  14 us
    pallas_call x2, Pallas kernels, join_call(): pl.pallas_call(join_kernel, out_shape=jax.ShapeDtypeStruct(rows.shape, ro...  4.77 us
    pallas_call x1, Pallas kernels, pack_call(): pl.pallas_call(functools.partial(pack_kernel, chips, width), out_shape=[j...  3.19 us
  transfers between devices with their start and end apart: 7, of which 4 were waited for; matrix products, arithmetic and copies ran while one was open for 0% of the time, Pallas kernels for 36%

profile of v1, /device:TPU:0, one launch (start us, length us, event | category | flops | bytes accessed | tf_op | source)
XLA Modules:
  0.0 152.9 jit_solution(14938478236323214726)
XLA Ops:
  0.6 3.2 %shard_map.84 = (bf16[16,4,128,128]{3,2,1,0:T(8,128)(2,1)}, bf16[16,3,128,128]{3,2,1,0:T(8,128)(2,1)}) custom-call(bf16[128,3072]{1,0:T(8,128)(2,1)} %q_ref.1, bf16[128,3072]{1,0:T(8,128)(2,1)} %k_ref.1, bf16[128,3072]{1,0:T(8,128)(2,1)} %v_ref.1, bf16[128,3072]{1,0:T(8,128)(2,1)} %g_ref.1), custom_call_target="tpu_custom_call" | custom-call | tf_op jit(solution)/shard_map/pallas_call | solution.py:323
  3.8 36.5 %all_to_all.20.own_ref = bf16[16,4,128,128]{3,2,1,0:T(8,128)(2,1)} all-to-all(bf16[16,4,128,128]{3,2,1,0:T(8,128)(2,1)} %get-tuple-element.17), channel_id=1, replica_groups={{0,2,4,6,8,10,12,14,16,18,20,22,24,26,28,30},{1,3,5,7,9,11,13,15,17,19,..., dimensions={0} | all-to-all | bytes 4194304 | tf_op jit(solution)/shard_map/all_to_all | solution.py:420
  40.3 0.0 collective-permute-start
  40.3 3.7 %all-to-all-start = ((bf16[16,3,128,128]{3,2,1,0:T(8,128)(2,1)}), bf16[16,3,128,128]{3,2,1,0:T(8,128)(2,1)S(1)}, u32[]{:S(2)}, u32[]{:S(2)}) async-start(bf16[16,3,128,128]{3,2,1,0:T(8,128)(2,1)} %get-tuple-element.16), calls=%async_computation | async-start | bytes 3145728 | tf_op jit(solution)/shard_map/all_to_all | solution.py:420
  44.0 0.8 collective-permute-done.oth_ref
  44.8 30.2 %shard_map.85 = (bf16[16,4,128,128]{3,2,1,0:T(8,128)(2,1)}, bf16[16,2,128,128]{3,2,1,0:T(8,128)(2,1)}, bf16[16,2,128,128]{3,2,1,0:T(8,128)(2,1)}) custom-call(s32[24,32,32]{2,1,0:T(8,128)} %masks_ref.3, bf16[16,4,128,128]{3,2,1,0:T(8,128)(2,1)} %all_to_all.20.own_ref, bf16[16,4,128,128]{3,2,1,0:T(8,128)(2,1)} %collective-permute-done.oth_ref), custom_call_target="tpu_custom_call" | custom-call | flops 12884901888 | bytes 8388608 | tf_op jit(solution)/shard_map/pallas_call | solution.py:209
  75.0 0.2 collective-permute-start.1
  75.3 0.0 all-to-all-done.refs_0_
  75.3 0.0 copy-start
  75.3 2.9 %collective-permute-done.1.taken_ref = bf16[16,2,128,128]{3,2,1,0:T(8,128)(2,1)} collective-permute-done((bf16[16,2,128,128]{3,2,1,0:T(8,128)(2,1)}, bf16[16,2,128,128]{3,2,1,0:T(8,128)(2,1)}, u32[]{:S(2)}, u32[]{:S(2)}) %collective-permute-start.1) | collective-permute-done | bytes 1048608 | tf_op jit(solution)/shard_map/ppermute | solution.py:424
  78.1 0.0 copy-done
  78.1 2.4 %shard_map.86.refs_1_ = bf16[16,4,128,128]{3,2,1,0:T(8,128)(2,1)} custom-call(bf16[16,4,128,128]{3,2,1,0:T(8,128)(2,1)} %get-tuple-element.18.rows_ref, bf16[16,2,128,128]{3,2,1,0:T(8,128)(2,1)} %get-tuple-element.19.keep_ref, bf16[16,2,128,128]{3,2,1,0:T(8,128)(2,1)} %collective-permute-done.1.taken_ref, ...), custom_call_target="tpu_custom_call", output_to_operand_aliasing={{}: (0, {})} | custom-call | tf_op jit(solution)/shard_map/pallas_call | solution.py:280
  80.5 0.2 collective-permute-start.2
  80.7 6.5 %all-to-all-start.2 = ((bf16[16,4,128,128]{3,2,1,0:T(8,128)(2,1)}), bf16[16,4,128,128]{3,2,1,0:T(8,128)(2,1)}, u32[]{:S(2)}, u32[]{:S(2)}) async-start(bf16[16,4,128,128]{3,2,1,0:T(8,128)(2,1)} %shard_map.86.refs_1_), calls=%async_computation.2 | async-start | bytes 4194304 | tf_op jit(solution)/shard_map/all_to_all | solution.py:420
  87.3 0.0 collective-permute-done.2.oth_ref
  87.3 21.9 %shard_map.88 = (bf16[16,3,128,128]{3,2,1,0:T(8,128)(2,1)}, bf16[16,2,128,128]{3,2,1,0:T(8,128)(2,1)}, bf16[16,2,128,128]{3,2,1,0:T(8,128)(2,1)}) custom-call(s32[24,32,32]{2,1,0:T(8,128)} %masks_ref.3, bf16[16,3,128,128]{3,2,1,0:T(8,128)(2,1)} %shard_map.87.own_ref, bf16[16,3,128,128]{3,2,1,0:T(8,128)(2,1)} %collective-permute-done.2.oth_ref), custom_call_target="tpu_custom_call" | custom-call | flops 6442450944 | bytes 8388608 | tf_op jit(solution)/shard_map/pallas_call | solution.py:209
  109.2 0.1 collective-permute-start.3
  109.3 11.6 %all-to-all-done.2.refs_0_.a_ref = bf16[16,4,128,128]{3,2,1,0:T(8,128)(2,1)} async-done(((bf16[16,4,128,128]{3,2,1,0:T(8,128)(2,1)}), bf16[16,4,128,128]{3,2,1,0:T(8,128)(2,1)}, u32[]{:S(2)}, u32[]{:S(2)}) %all-to-all-start.2) | async-done | bytes 2097184 | tf_op jit(solution)/shard_map/all_to_all | solution.py:420
  120.9 0.0 collective-permute-done.3.taken_ref
  120.9 0.0 copy-start.1
  120.9 1.0 copy-done.1
  121.8 2.4 %shard_map.89 = bf16[16,3,128,128]{3,2,1,0:T(8,128)(2,1)} custom-call(bf16[16,3,128,128]{3,2,1,0:T(8,128)(2,1)} %get-tuple-element.21.rows_ref, bf16[16,2,128,128]{3,2,1,0:T(8,128)(2,1)} %get-tuple-element.22.keep_ref, bf16[16,2,128,128]{3,2,1,0:T(8,128)(2,1)} %copy-done.1, ...), custom_call_target="tpu_custom_call", output_to_operand_aliasing={{}: (0, {})} | custom-call | tf_op jit(solution)/shard_map/pallas_call | solution.py:280
  124.2 3.7 %all-to-all-start.3 = ((bf16[16,3,128,128]{3,2,1,0:T(8,128)(2,1)}), bf16[16,3,128,128]{3,2,1,0:T(8,128)(2,1)S(1)}, u32[]{:S(2)}, u32[]{:S(2)}) async-start(bf16[16,3,128,128]{3,2,1,0:T(8,128)(2,1)} %shard_map.89), calls=%async_computation.3 | async-start | bytes 3145728 | tf_op jit(solution)/shard_map/all_to_all | solution.py:420
  128.0 2.6 %shard_map.90 = (bf16[128,3072]{1,0:T(8,128)(2,1)}, bf16[128,3072]{1,0:T(8,128)(2,1)}, bf16[128,3072]{1,0:T(8,128)(2,1)}, bf16[128,3072]{1,0:T(8,128)(2,1)}) custom-call(bf16[16,4,128,128]{3,2,1,0:T(8,128)(2,1)} %all-to-all-done.2.refs_0_.a_ref), custom_call_target="tpu_custom_call" | custom-call | tf_op jit(solution)/shard_map/pallas_call | solution.py:380
  130.5 21.1 %all-to-all-done.3.b_ref = bf16[16,3,128,128]{3,2,1,0:T(8,128)(2,1)S(1)} async-done(((bf16[16,3,128,128]{3,2,1,0:T(8,128)(2,1)}), bf16[16,3,128,128]{3,2,1,0:T(8,128)(2,1)S(1)}, u32[]{:S(2)}, u32[]{:S(2)}) %all-to-all-start.3) | async-done | bytes 1572896 | tf_op jit(solution)/shard_map/all_to_all | solution.py:420
  151.6 1.1 shard_map.91
  (1 shorter events, 0.0 us)
Async XLA Ops:
  40.3 4.5 %collective-permute-start = (bf16[16,4,128,128]{3,2,1,0:T(8,128)(2,1)}, bf16[16,4,128,128]{3,2,1,0:T(8,128)(2,1)}, u32[]{:S(2)}, u32[]{:S(2)}) collective-permute-start(bf16[16,4,128,128]{3,2,1,0:T(8,128)(2,1)} %all_to_all.20.own_ref), channel_id=1, source_target_pairs={{0,1},{1,0},{2,3},{3,2},{4,5},{5,4},{6,7},{7,6},{8,9},{9,8},{10,11... | collective-permute-start | bytes 6291464 | tf_op jit(solution)/shard_map/ppermute | solution.py:430
  40.3 35.0 %all-to-all-start = ((bf16[16,3,128,128]{3,2,1,0:T(8,128)(2,1)}), bf16[16,3,128,128]{3,2,1,0:T(8,128)(2,1)S(1)}, u32[]{:S(2)}, u32[]{:S(2)}) async-start(bf16[16,3,128,128]{3,2,1,0:T(8,128)(2,1)} %get-tuple-element.16), calls=%async_computation | async-start | bytes 3145728 | tf_op jit(solution)/shard_map/all_to_all | solution.py:420
  75.0 3.1 %collective-permute-start.1 = (bf16[16,2,128,128]{3,2,1,0:T(8,128)(2,1)}, bf16[16,2,128,128]{3,2,1,0:T(8,128)(2,1)}, u32[]{:S(2)}, u32[]{:S(2)}) collective-permute-start(bf16[16,2,128,128]{3,2,1,0:T(8,128)(2,1)} %get-tuple-element.20), channel_id=1, source_target_pairs={{0,1},{1,0},{2,3},{3,2},{4,5},{5,4},{6,7},{7,6},{8,9},{9,8},{10,11... | collective-permute-start | bytes 3145736 | tf_op jit(solution)/shard_map/ppermute | solution.py:424
  75.3 2.9 %copy-start = (bf16[16,3,128,128]{3,2,1,0:T(8,128)(2,1)}, bf16[16,3,128,128]{3,2,1,0:T(8,128)(2,1)S(1)}, u32[]{:S(2)}) copy-start(bf16[16,3,128,128]{3,2,1,0:T(8,128)(2,1)S(1)} %all-to-all-done.refs_0_) | copy-start | bytes 4718596
  80.5 6.8 %collective-permute-start.2 = (bf16[16,3,128,128]{3,2,1,0:T(8,128)(2,1)}, bf16[16,3,128,128]{3,2,1,0:T(8,128)(2,1)}, u32[]{:S(2)}, u32[]{:S(2)}) collective-permute-start(bf16[16,3,128,128]{3,2,1,0:T(8,128)(2,1)} %shard_map.87.own_ref), channel_id=1, source_target_pairs={{0,1},{1,0},{2,3},{3,2},{4,5},{5,4},{6,7},{7,6},{8,9},{9,8},{10,11... | collective-permute-start | bytes 4718600 | tf_op jit(solution)/shard_map/ppermute | solution.py:433
  80.7 40.1 %all-to-all-start.2 = ((bf16[16,4,128,128]{3,2,1,0:T(8,128)(2,1)}), bf16[16,4,128,128]{3,2,1,0:T(8,128)(2,1)}, u32[]{:S(2)}, u32[]{:S(2)}) async-start(bf16[16,4,128,128]{3,2,1,0:T(8,128)(2,1)} %shard_map.86.refs_1_), calls=%async_computation.2 | async-start | bytes 4194304 | tf_op jit(solution)/shard_map/all_to_all | solution.py:420
  109.2 11.7 %collective-permute-start.3 = (bf16[16,2,128,128]{3,2,1,0:T(8,128)(2,1)}, bf16[16,2,128,128]{3,2,1,0:T(8,128)(2,1)S(1)}, u32[]{:S(2)}, u32[]{:S(2)}) collective-permute-start(bf16[16,2,128,128]{3,2,1,0:T(8,128)(2,1)} %get-tuple-element.23), channel_id=1, source_target_pairs={{0,1},{1,0},{2,3},{3,2},{4,5},{5,4},{6,7},{7,6},{8,9},{9,8},{10,11... | collective-permute-start | bytes 3145736 | tf_op jit(solution)/shard_map/ppermute | solution.py:424
  120.9 1.0 copy-start.1
  124.2 27.4 %all-to-all-start.3 = ((bf16[16,3,128,128]{3,2,1,0:T(8,128)(2,1)}), bf16[16,3,128,128]{3,2,1,0:T(8,128)(2,1)S(1)}, u32[]{:S(2)}, u32[]{:S(2)}) async-start(bf16[16,3,128,128]{3,2,1,0:T(8,128)(2,1)} %shard_map.89), calls=%async_computation.3 | async-start | bytes 3145728 | tf_op jit(solution)/shard_map/all_to_all | solution.py:420

commit v2 on v1

--- a/solution.py
+++ b/solution.py
@@ -9,6 +9,7 @@
 
 LANES = 512
 BLOCK = 512
+GROUP = 4096
 STEPS_WHOLE = (4096, 4096, 4096, 4096, 4096)
 STEPS_SPLIT = (512, 512, 512, 512, 512)
 NT = (((1,), (1,)), ((), ()))
@@ -25,7 +26,7 @@
 ):
     send_ref, keep_ref, give_ref = refs[depends : depends + 3]
     (rows_scr, qg_scr, k_scr, v_scr, kt_scr, vt_scr, dk_scr, dv_scr, x_scr, p_scr, bias_scr, mask_scr) = refs[depends + 3 : depends + 15]
-    (top_scr, qn_scr, gn_scr, stat_scr, give_scr, keep_scr, sems) = refs[depends + 15 :]
+    (top_scr, stat_scr, give_scr, keep_scr, sems) = refs[depends + 15 :]
     half, slots, tile, width = own_ref.shape
     blocks = 2 * half
     keys = blocks * tile
@@ -94,30 +95,29 @@
         if scores:
             q_next = q_tile(t + 1)
         if grads:
-            g, qn, gn = g_tile(t - 1), qn_scr[...], gn_scr[...]
-            delta, rl_last = stat_scr[0:1, :], stat_scr[1:2, :]
+            g, q = g_tile(t - 1), q_tile(t - 1)
+            delta, inverse = stat_scr[0:1, :], stat_scr[1:2, :].astype(bf16)
         if probs:
             top = jnp.max(top_scr[...], axis=0, keepdims=True) * c2
 
         def step(i, carry):
             best, o, dq = carry
-            at = pl.ds(at_multiple(i * step_rows, step_rows), step_rows)
-            ds_all, p_all = [], []
+            group = min(GROUP, step_rows)
+            ds_all = []
             for u in range(subs):
                 first = i * step_rows + u * BLOCK
                 sub = pl.ds(at_multiple(first, BLOCK), BLOCK)
                 pair = pl.ds(i * (step_rows // tile) + u * (BLOCK // tile), BLOCK // tile)
                 if grads:
-                    pb = p_scr[sub, :]
+                    pb = p_scr[sub, :] * inverse
                     dp = dot(v_scr[pair].reshape(BLOCK, width), g, NT)
                     ds = pb * (dp - delta).astype(bf16)
-                    dv_scr[sub, :] += dot(pb, gn)
-                    dk_scr[sub, :] += dot(ds, qn)
+                    dv_scr[sub, :] += dot(pb, g)
+                    dk_scr[sub, :] += dot(ds, q)
                     ds_all.append(ds)
                 if probs:
                     pb = jnp.exp2(x_scr[sub, :] * c2 - top).astype(bf16)
                     p_scr[sub, :] = pb
-                    p_all.append(pb)
                 if scores:
                     s = dot(k_scr[pair].reshape(BLOCK, width), q_next, NT).reshape(BLOCK // tile, tile, lanes)
                     for w in range(BLOCK // tile):
@@ -133,10 +133,13 @@
                         vt_scr[width:, to] = jnp.ones((tall - width, tile), bf16)
                         dk_scr[to, :] = jnp.zeros((tile, width), f32)
                         dv_scr[to, :] = jnp.zeros((tile, width), f32)
-            if grads:
-                dq = dq + dot(kt_scr[:, at], jnp.concatenate(ds_all, 0))
-            if probs:
-                o = o + dot(vt_scr[:, at], jnp.concatenate(p_all, 0))
+                if (u + 1) * BLOCK % group == 0:
+                    at = pl.ds(at_multiple(first + BLOCK - group, group), group)
+                    if grads:
+                        dq = dq + dot(kt_scr[:, at], jnp.concatenate(ds_all, 0))
+                        ds_all = []
+                    if probs:
+                        o = o + dot(vt_scr[:, at], p_scr[at, :])
             return best, o, dq
 
         start = (
@@ -151,7 +154,7 @@
         if scores:
             top_scr[...] = best
         if grads:
-            put(t - 1, 1, (dq * (rl_last * scale)).T)
+            put(t - 1, 1, (dq * scale).T)
         if probs:
             rl = 1.0 / o[width : width + 1]
             ot = o[:width] * rl
@@ -159,9 +162,6 @@
             gf = g_tile(t).astype(f32)
             stat_scr[0:1, :] = jnp.sum(gf.T * ot, axis=0, keepdims=True)
             stat_scr[1:2, :] = rl
-            column = jnp.broadcast_to(rl, (width, lanes)).T
-            qn_scr[...] = (q_tile(t).astype(f32) * column).astype(bf16)
-            gn_scr[...] = (gf * column).astype(bf16)
 
     stage(-1, True, False, False, steps[0])
     stage(0, True, True, False, steps[1])
@@ -229,8 +229,6 @@
             pltpu.VMEM((rows // lanes, 2 * half, lanes), f32),
             pltpu.VMEM((2 * half, 2 * half), jnp.int32),
             pltpu.VMEM((8, lanes), f32),
-            pltpu.VMEM((lanes, width), bf16),
-            pltpu.VMEM((lanes, width), bf16),
             pltpu.VMEM((8, lanes), f32),
             pltpu.VMEM((half, 2, tile, width), bf16),
             pltpu.VMEM((half, 2, tile, width), bf16),
@@ -433,7 +431,9 @@
     other_b = lax.ppermute(got_b, "seq", swap)
     parts_b = attend_call(masks, got_b, other_b, (), True)
     back_a = exchange(send_a)
-    back_b = exchange(gather(parts_b, back_a, 56 * 2**20))
+    rows, keep, give = parts_b
+    send_b = join_call(rows, keep, lax.ppermute(give, "seq", swap), (), 62 * 2**20)
+    back_b = exchange(after(send_b, back_a))
     return tuple(unpack_call(back_a, back_b, heads))
 
 

time: 153 us -> 150 us (0.980)
  waiting for transfers between devices: 36.3 us -> 33.1 us
    all_to_all x3, waiting for transfers between devices: 32.7 us -> 26.6 us  [exchange(): lax.all_to_all(array, 'seq', 0, 0, axis_index_groups=groups, tiled=True)]
    ppermute x0 -> x1, waiting for transfers between devices: none -> 2.86 us  [body(): lax.ppermute(give, 'seq', swap)]
  transfers between devices with their start and end apart: 7 -> 7, of which waited for: 4 -> 5; matrix products, arithmetic and copies ran while one was open for 0% -> 0% of each run, Pallas kernels for 36% -> 38%
where the time goes in v2:
time: 150 us; the launch traced here: 149 us
  Pallas kernels  63.2 us (42%)
  blocking collectives  36.5 us (24%)
  waiting for transfers between devices  33.1 us (22%)
  starting transfers between devices  14.5 us (10%)
    pallas_call x2, Pallas kernels, attend_call(): pl.pallas_call(functools.partial(attend_kernel, STEPS_SPLIT if split else...  51.6 us
    all_to_all x1, blocking collectives, exchange(): lax.all_to_all(array, 'seq', 0, 0, axis_index_groups=groups, tiled=True)  36.5 us
    all_to_all x3, waiting for transfers between devices, exchange(): lax.all_to_all(array, 'seq', 0, 0, axis_index_groups=groups, tiled=True)  26.6 us
    all_to_all x3, starting transfers between devices, exchange(): lax.all_to_all(array, 'seq', 0, 0, axis_index_groups=groups, tiled=True)  13.9 us
    pallas_call x2, Pallas kernels, join_call(): pl.pallas_call(join_kernel, out_shape=jax.ShapeDtypeStruct(rows.shape, ro...  4.76 us
    pallas_call x1, Pallas kernels, pack_call(): pl.pallas_call(functools.partial(pack_kernel, chips, width), out_shape=[j...  3.19 us
  transfers between devices with their start and end apart: 7, of which 5 were waited for; matrix products, arithmetic and copies ran while one was open for 0% of the time, Pallas kernels for 38%

profile of v2, /device:TPU:0, one launch (start us, length us, event | category | flops | bytes accessed | tf_op | source)
XLA Modules:
  0.0 149.1 jit_solution(2169082998567635594)
XLA Ops:
  0.6 3.2 %shard_map.84 = (bf16[16,4,128,128]{3,2,1,0:T(8,128)(2,1)}, bf16[16,3,128,128]{3,2,1,0:T(8,128)(2,1)}) custom-call(bf16[128,3072]{1,0:T(8,128)(2,1)} %q_ref.1, bf16[128,3072]{1,0:T(8,128)(2,1)} %k_ref.1, bf16[128,3072]{1,0:T(8,128)(2,1)} %v_ref.1, bf16[128,3072]{1,0:T(8,128)(2,1)} %g_ref.1), custom_call_target="tpu_custom_call" | custom-call | tf_op jit(solution)/shard_map/pallas_call | solution.py:321
  3.8 36.5 %all_to_all.20.own_ref = bf16[16,4,128,128]{3,2,1,0:T(8,128)(2,1)} all-to-all(bf16[16,4,128,128]{3,2,1,0:T(8,128)(2,1)} %get-tuple-element.17), channel_id=1, replica_groups={{0,2,4,6,8,10,12,14,16,18,20,22,24,26,28,30},{1,3,5,7,9,11,13,15,17,19,..., dimensions={0} | all-to-all | bytes 4194304 | tf_op jit(solution)/shard_map/all_to_all | solution.py:418
  40.3 0.0 collective-permute-start
  40.3 3.7 %all-to-all-start = ((bf16[16,3,128,128]{3,2,1,0:T(8,128)(2,1)}), bf16[16,3,128,128]{3,2,1,0:T(8,128)(2,1)S(1)}, u32[]{:S(2)}, u32[]{:S(2)}) async-start(bf16[16,3,128,128]{3,2,1,0:T(8,128)(2,1)} %get-tuple-element.16), calls=%async_computation | async-start | bytes 3145728 | tf_op jit(solution)/shard_map/all_to_all | solution.py:418
  44.0 0.8 collective-permute-done.oth_ref
  44.8 29.8 %shard_map.85 = (bf16[16,4,128,128]{3,2,1,0:T(8,128)(2,1)}, bf16[16,2,128,128]{3,2,1,0:T(8,128)(2,1)}, bf16[16,2,128,128]{3,2,1,0:T(8,128)(2,1)}) custom-call(s32[24,32,32]{2,1,0:T(8,128)} %masks_ref.3, bf16[16,4,128,128]{3,2,1,0:T(8,128)(2,1)} %all_to_all.20.own_ref, bf16[16,4,128,128]{3,2,1,0:T(8,128)(2,1)} %collective-permute-done.oth_ref), custom_call_target="tpu_custom_call" | custom-call | flops 12884901888 | bytes 8388608 | tf_op jit(solution)/shard_map/pallas_call | solution.py:209
  74.6 0.2 collective-permute-start.1
  74.9 0.0 all-to-all-done.refs_0_
  74.9 0.0 copy-start
  74.9 2.8 %collective-permute-done.1.taken_ref = bf16[16,2,128,128]{3,2,1,0:T(8,128)(2,1)} collective-permute-done((bf16[16,2,128,128]{3,2,1,0:T(8,128)(2,1)}, bf16[16,2,128,128]{3,2,1,0:T(8,128)(2,1)}, u32[]{:S(2)}, u32[]{:S(2)}) %collective-permute-start.1) | collective-permute-done | bytes 1048608 | tf_op jit(solution)/shard_map/ppermute | solution.py:422
  77.7 0.0 copy-done
  77.7 2.4 %shard_map.86.refs_1_ = bf16[16,4,128,128]{3,2,1,0:T(8,128)(2,1)} custom-call(bf16[16,4,128,128]{3,2,1,0:T(8,128)(2,1)} %get-tuple-element.18.rows_ref, bf16[16,2,128,128]{3,2,1,0:T(8,128)(2,1)} %get-tuple-element.19.keep_ref, bf16[16,2,128,128]{3,2,1,0:T(8,128)(2,1)} %collective-permute-done.1.taken_ref, ...), custom_call_target="tpu_custom_call", output_to_operand_aliasing={{}: (0, {})} | custom-call | tf_op jit(solution)/shard_map/pallas_call | solution.py:278
  80.1 0.2 collective-permute-start.2
  80.4 6.5 %all-to-all-start.2 = ((bf16[16,4,128,128]{3,2,1,0:T(8,128)(2,1)}), bf16[16,4,128,128]{3,2,1,0:T(8,128)(2,1)}, u32[]{:S(2)}, u32[]{:S(2)}) async-start(bf16[16,4,128,128]{3,2,1,0:T(8,128)(2,1)} %shard_map.86.refs_1_), calls=%async_computation.2 | async-start | bytes 4194304 | tf_op jit(solution)/shard_map/all_to_all | solution.py:418
  86.9 0.0 collective-permute-done.2.oth_ref
  86.9 21.8 %shard_map.88 = (bf16[16,3,128,128]{3,2,1,0:T(8,128)(2,1)}, bf16[16,2,128,128]{3,2,1,0:T(8,128)(2,1)}, bf16[16,2,128,128]{3,2,1,0:T(8,128)(2,1)}) custom-call(s32[24,32,32]{2,1,0:T(8,128)} %masks_ref.3, bf16[16,3,128,128]{3,2,1,0:T(8,128)(2,1)} %shard_map.87.own_ref, bf16[16,3,128,128]{3,2,1,0:T(8,128)(2,1)} %collective-permute-done.2.oth_ref), custom_call_target="tpu_custom_call" | custom-call | flops 6442450944 | bytes 8388608 | tf_op jit(solution)/shard_map/pallas_call | solution.py:209
  108.7 0.1 collective-permute-start.3
  108.8 2.9 %collective-permute-done.3.taken_ref = bf16[16,2,128,128]{3,2,1,0:T(8,128)(2,1)S(1)} collective-permute-done((bf16[16,2,128,128]{3,2,1,0:T(8,128)(2,1)}, bf16[16,2,128,128]{3,2,1,0:T(8,128)(2,1)S(1)}, u32[]{:S(2)}, u32[]{:S(2)}) %collective-permute-start.3) | collective-permute-done | bytes 1048608 | tf_op jit(solution)/shard_map/ppermute | solution.py:435
  111.6 0.0 copy-start.1
  111.6 1.0 copy-done.1
  112.6 2.4 %shard_map.89.refs_0_ = bf16[16,3,128,128]{3,2,1,0:T(8,128)(2,1)} custom-call(bf16[16,3,128,128]{3,2,1,0:T(8,128)(2,1)} %get-tuple-element.21.rows_ref, bf16[16,2,128,128]{3,2,1,0:T(8,128)(2,1)} %get-tuple-element.22.keep_ref, bf16[16,2,128,128]{3,2,1,0:T(8,128)(2,1)} %copy-done.1), custom_call_target="tpu_custom_call", output_to_operand_aliasing={{}: (0, {})} | custom-call | tf_op jit(solution)/shard_map/pallas_call | solution.py:278
  115.0 5.5 %all-to-all-done.2.refs_1_.a_ref = bf16[16,4,128,128]{3,2,1,0:T(8,128)(2,1)} async-done(((bf16[16,4,128,128]{3,2,1,0:T(8,128)(2,1)}), bf16[16,4,128,128]{3,2,1,0:T(8,128)(2,1)}, u32[]{:S(2)}, u32[]{:S(2)}) %all-to-all-start.2) | async-done | bytes 2097184 | tf_op jit(solution)/shard_map/all_to_all | solution.py:418
  120.5 3.7 %all-to-all-start.3 = ((bf16[16,3,128,128]{3,2,1,0:T(8,128)(2,1)}), bf16[16,3,128,128]{3,2,1,0:T(8,128)(2,1)S(1)}, u32[]{:S(2)}, u32[]{:S(2)}) async-start(bf16[16,3,128,128]{3,2,1,0:T(8,128)(2,1)} %shard_map.90), calls=%async_computation.3 | async-start | bytes 3145728 | tf_op jit(solution)/shard_map/all_to_all | solution.py:418
  124.2 2.6 %shard_map.91 = (bf16[128,3072]{1,0:T(8,128)(2,1)}, bf16[128,3072]{1,0:T(8,128)(2,1)}, bf16[128,3072]{1,0:T(8,128)(2,1)}, bf16[128,3072]{1,0:T(8,128)(2,1)}) custom-call(bf16[16,4,128,128]{3,2,1,0:T(8,128)(2,1)} %all-to-all-done.2.refs_1_.a_ref), custom_call_target="tpu_custom_call" | custom-call | tf_op jit(solution)/shard_map/pallas_call | solution.py:378
  126.8 21.1 %all-to-all-done.3.b_ref = bf16[16,3,128,128]{3,2,1,0:T(8,128)(2,1)S(1)} async-done(((bf16[16,3,128,128]{3,2,1,0:T(8,128)(2,1)}), bf16[16,3,128,128]{3,2,1,0:T(8,128)(2,1)S(1)}, u32[]{:S(2)}, u32[]{:S(2)}) %all-to-all-start.3) | async-done | bytes 1572896 | tf_op jit(solution)/shard_map/all_to_all | solution.py:418
  147.9 1.1 shard_map.92
  (2 shorter events, 0.0 us)
Async XLA Ops:
  40.3 4.5 %collective-permute-start = (bf16[16,4,128,128]{3,2,1,0:T(8,128)(2,1)}, bf16[16,4,128,128]{3,2,1,0:T(8,128)(2,1)}, u32[]{:S(2)}, u32[]{:S(2)}) collective-permute-start(bf16[16,4,128,128]{3,2,1,0:T(8,128)(2,1)} %all_to_all.20.own_ref), channel_id=1, source_target_pairs={{0,1},{1,0},{2,3},{3,2},{4,5},{5,4},{6,7},{7,6},{8,9},{9,8},{10,11... | collective-permute-start | bytes 6291464 | tf_op jit(solution)/shard_map/ppermute | solution.py:428
  40.3 34.6 %all-to-all-start = ((bf16[16,3,128,128]{3,2,1,0:T(8,128)(2,1)}), bf16[16,3,128,128]{3,2,1,0:T(8,128)(2,1)S(1)}, u32[]{:S(2)}, u32[]{:S(2)}) async-start(bf16[16,3,128,128]{3,2,1,0:T(8,128)(2,1)} %get-tuple-element.16), calls=%async_computation | async-start | bytes 3145728 | tf_op jit(solution)/shard_map/all_to_all | solution.py:418
  74.6 3.1 %collective-permute-start.1 = (bf16[16,2,128,128]{3,2,1,0:T(8,128)(2,1)}, bf16[16,2,128,128]{3,2,1,0:T(8,128)(2,1)}, u32[]{:S(2)}, u32[]{:S(2)}) collective-permute-start(bf16[16,2,128,128]{3,2,1,0:T(8,128)(2,1)} %get-tuple-element.20), channel_id=1, source_target_pairs={{0,1},{1,0},{2,3},{3,2},{4,5},{5,4},{6,7},{7,6},{8,9},{9,8},{10,11... | collective-permute-start | bytes 3145736 | tf_op jit(solution)/shard_map/ppermute | solution.py:422
  74.9 2.9 %copy-start = (bf16[16,3,128,128]{3,2,1,0:T(8,128)(2,1)}, bf16[16,3,128,128]{3,2,1,0:T(8,128)(2,1)S(1)}, u32[]{:S(2)}) copy-start(bf16[16,3,128,128]{3,2,1,0:T(8,128)(2,1)S(1)} %all-to-all-done.refs_0_) | copy-start | bytes 4718596
  80.1 6.8 %collective-permute-start.2 = (bf16[16,3,128,128]{3,2,1,0:T(8,128)(2,1)}, bf16[16,3,128,128]{3,2,1,0:T(8,128)(2,1)}, u32[]{:S(2)}, u32[]{:S(2)}) collective-permute-start(bf16[16,3,128,128]{3,2,1,0:T(8,128)(2,1)} %shard_map.87.own_ref), channel_id=1, source_target_pairs={{0,1},{1,0},{2,3},{3,2},{4,5},{5,4},{6,7},{7,6},{8,9},{9,8},{10,11... | collective-permute-start | bytes 4718600 | tf_op jit(solution)/shard_map/ppermute | solution.py:431
  80.4 40.1 %all-to-all-start.2 = ((bf16[16,4,128,128]{3,2,1,0:T(8,128)(2,1)}), bf16[16,4,128,128]{3,2,1,0:T(8,128)(2,1)}, u32[]{:S(2)}, u32[]{:S(2)}) async-start(bf16[16,4,128,128]{3,2,1,0:T(8,128)(2,1)} %shard_map.86.refs_1_), calls=%async_computation.2 | async-start | bytes 4194304 | tf_op jit(solution)/shard_map/all_to_all | solution.py:418
  108.7 3.0 %collective-permute-start.3 = (bf16[16,2,128,128]{3,2,1,0:T(8,128)(2,1)}, bf16[16,2,128,128]{3,2,1,0:T(8,128)(2,1)S(1)}, u32[]{:S(2)}, u32[]{:S(2)}) collective-permute-start(bf16[16,2,128,128]{3,2,1,0:T(8,128)(2,1)} %get-tuple-element.23), channel_id=1, source_target_pairs={{0,1},{1,0},{2,3},{3,2},{4,5},{5,4},{6,7},{7,6},{8,9},{9,8},{10,11... | collective-permute-start | bytes 3145736 | tf_op jit(solution)/shard_map/ppermute | solution.py:435
  111.6 1.0 copy-start.1
  120.5 27.4 %all-to-all-start.3 = ((bf16[16,3,128,128]{3,2,1,0:T(8,128)(2,1)}), bf16[16,3,128,128]{3,2,1,0:T(8,128)(2,1)S(1)}, u32[]{:S(2)}, u32[]{:S(2)}) async-start(bf16[16,3,128,128]{3,2,1,0:T(8,128)(2,1)} %shard_map.90), calls=%async_computation.3 | async-start | bytes 3145728 | tf_op jit(solution)/shard_map/all_to_all | solution.py:418

commit v3 on v2

--- a/solution.py
+++ b/solution.py
@@ -8,7 +8,8 @@
 from jax.sharding import PartitionSpec as P
 
 LANES = 512
-BLOCK = 512
+BLOCK_WHOLE = 256
+BLOCK_SPLIT = 512
 GROUP = 4096
 STEPS_WHOLE = (4096, 4096, 4096, 4096, 4096)
 STEPS_SPLIT = (512, 512, 512, 512, 512)
@@ -91,7 +92,8 @@
 
     def stage(t, scores, probs, grads, step_rows):
         prepare = not probs and not grads
-        subs = step_rows // BLOCK
+        block = BLOCK_SPLIT if split else BLOCK_WHOLE
+        subs = step_rows // block
         if scores:
             q_next = q_tile(t + 1)
         if grads:
@@ -105,12 +107,12 @@
             group = min(GROUP, step_rows)
             ds_all = []
             for u in range(subs):
-                first = i * step_rows + u * BLOCK
-                sub = pl.ds(at_multiple(first, BLOCK), BLOCK)
-                pair = pl.ds(i * (step_rows // tile) + u * (BLOCK // tile), BLOCK // tile)
+                first = i * step_rows + u * block
+                sub = pl.ds(at_multiple(first, block), block)
+                pair = pl.ds(i * (step_rows // tile) + u * (block // tile), block // tile)
                 if grads:
                     pb = p_scr[sub, :] * inverse
-                    dp = dot(v_scr[pair].reshape(BLOCK, width), g, NT)
+                    dp = dot(v_scr[pair].reshape(block, width), g, NT)
                     ds = pb * (dp - delta).astype(bf16)
                     dv_scr[sub, :] += dot(pb, g)
                     dk_scr[sub, :] += dot(ds, q)
@@ -119,22 +121,22 @@
                     pb = jnp.exp2(x_scr[sub, :] * c2 - top).astype(bf16)
                     p_scr[sub, :] = pb
                 if scores:
-                    s = dot(k_scr[pair].reshape(BLOCK, width), q_next, NT).reshape(BLOCK // tile, tile, lanes)
-                    for w in range(BLOCK // tile):
-                        x = s[w] + bias_scr[t + 1, pl.ds(i * (step_rows // tile) + u * (BLOCK // tile) + w, 1), :]
+                    s = dot(k_scr[pair].reshape(block, width), q_next, NT).reshape(block // tile, tile, lanes)
+                    for w in range(block // tile):
+                        x = s[w] + bias_scr[t + 1, pl.ds(i * (step_rows // tile) + u * (block // tile) + w, 1), :]
                         x_scr[pl.ds(at_multiple(first + w * tile, tile), tile), :] = x
                         best = jnp.maximum(best, jnp.max(x.reshape(tile // 8, 8, lanes), axis=0))
                 if prepare:
-                    for w in range(BLOCK // tile):
-                        j = i * (step_rows // tile) + u * (BLOCK // tile) + w
+                    for w in range(block // tile):
+                        j = i * (step_rows // tile) + u * (block // tile) + w
                         to = pl.ds(at_multiple(first + w * tile, tile), tile)
                         kt_scr[:, to] = k_scr[j].T
                         vt_scr[0:width, to] = v_scr[j].T
                         vt_scr[width:, to] = jnp.ones((tall - width, tile), bf16)
                         dk_scr[to, :] = jnp.zeros((tile, width), f32)
                         dv_scr[to, :] = jnp.zeros((tile, width), f32)
-                if (u + 1) * BLOCK % group == 0:
-                    at = pl.ds(at_multiple(first + BLOCK - group, group), group)
+                if (u + 1) * block % group == 0:
+                    at = pl.ds(at_multiple(first + block - group, group), group)
                     if grads:
                         dq = dq + dot(kt_scr[:, at], jnp.concatenate(ds_all, 0))
                         ds_all = []

time: 150 us -> 149 us (level)
  no operation moved by 1% of the time
where the time goes in v3:
time: 149 us
  Pallas kernels  62.7 us (42%)
  blocking collectives  36.5 us (24%)
  waiting for transfers between devices  33.2 us (22%)
  starting transfers between devices  14.5 us (10%)
    pallas_call x2, Pallas kernels, attend_call(): pl.pallas_call(functools.partial(attend_kernel, STEPS_SPLIT if split else...  51.2 us
    all_to_all x1, blocking collectives, exchange(): lax.all_to_all(array, 'seq', 0, 0, axis_index_groups=groups, tiled=True)  36.5 us
    all_to_all x3, waiting for transfers between devices, exchange(): lax.all_to_all(array, 'seq', 0, 0, axis_index_groups=groups, tiled=True)  26.6 us
    all_to_all x3, starting transfers between devices, exchange(): lax.all_to_all(array, 'seq', 0, 0, axis_index_groups=groups, tiled=True)  13.9 us
    pallas_call x2, Pallas kernels, join_call(): pl.pallas_call(join_kernel, out_shape=jax.ShapeDtypeStruct(rows.shape, ro...  4.76 us
    pallas_call x1, Pallas kernels, pack_call(): pl.pallas_call(functools.partial(pack_kernel, chips, width), out_shape=[j...  3.19 us
  transfers between devices with their start and end apart: 7, of which 5 were waited for; matrix products, arithmetic and copies ran while one was open for 0% of the time, Pallas kernels for 38%

profile of v3, /device:TPU:0, one launch (start us, length us, event | category | flops | bytes accessed | tf_op | source)
XLA Modules:
  0.0 148.7 jit_solution(12773257214467190964)
XLA Ops:
  0.6 3.2 %shard_map.84 = (bf16[16,4,128,128]{3,2,1,0:T(8,128)(2,1)}, bf16[16,3,128,128]{3,2,1,0:T(8,128)(2,1)}) custom-call(bf16[128,3072]{1,0:T(8,128)(2,1)} %q_ref.1, bf16[128,3072]{1,0:T(8,128)(2,1)} %k_ref.1, bf16[128,3072]{1,0:T(8,128)(2,1)} %v_ref.1, bf16[128,3072]{1,0:T(8,128)(2,1)} %g_ref.1), custom_call_target="tpu_custom_call" | custom-call | tf_op jit(solution)/shard_map/pallas_call | solution.py:323
  3.8 36.5 %all_to_all.20.own_ref = bf16[16,4,128,128]{3,2,1,0:T(8,128)(2,1)} all-to-all(bf16[16,4,128,128]{3,2,1,0:T(8,128)(2,1)} %get-tuple-element.17), channel_id=1, replica_groups={{0,2,4,6,8,10,12,14,16,18,20,22,24,26,28,30},{1,3,5,7,9,11,13,15,17,19,..., dimensions={0} | all-to-all | bytes 4194304 | tf_op jit(solution)/shard_map/all_to_all | solution.py:420
  40.3 0.0 collective-permute-start
  40.3 3.7 %all-to-all-start = ((bf16[16,3,128,128]{3,2,1,0:T(8,128)(2,1)}), bf16[16,3,128,128]{3,2,1,0:T(8,128)(2,1)S(1)}, u32[]{:S(2)}, u32[]{:S(2)}) async-start(bf16[16,3,128,128]{3,2,1,0:T(8,128)(2,1)} %get-tuple-element.16), calls=%async_computation | async-start | bytes 3145728 | tf_op jit(solution)/shard_map/all_to_all | solution.py:420
  44.0 0.8 collective-permute-done.oth_ref
  44.8 29.4 %shard_map.85 = (bf16[16,4,128,128]{3,2,1,0:T(8,128)(2,1)}, bf16[16,2,128,128]{3,2,1,0:T(8,128)(2,1)}, bf16[16,2,128,128]{3,2,1,0:T(8,128)(2,1)}) custom-call(s32[24,32,32]{2,1,0:T(8,128)} %masks_ref.3, bf16[16,4,128,128]{3,2,1,0:T(8,128)(2,1)} %all_to_all.20.own_ref, bf16[16,4,128,128]{3,2,1,0:T(8,128)(2,1)} %collective-permute-done.oth_ref), custom_call_target="tpu_custom_call" | custom-call | flops 12884901888 | bytes 8388608 | tf_op jit(solution)/shard_map/pallas_call | solution.py:211
  74.2 0.2 collective-permute-start.1
  74.4 0.0 all-to-all-done.refs_0_
  74.4 0.0 copy-start
  74.4 2.9 %collective-permute-done.1.taken_ref = bf16[16,2,128,128]{3,2,1,0:T(8,128)(2,1)} collective-permute-done((bf16[16,2,128,128]{3,2,1,0:T(8,128)(2,1)}, bf16[16,2,128,128]{3,2,1,0:T(8,128)(2,1)}, u32[]{:S(2)}, u32[]{:S(2)}) %collective-permute-start.1) | collective-permute-done | bytes 1048608 | tf_op jit(solution)/shard_map/ppermute | solution.py:424
  77.3 0.0 copy-done
  77.3 2.4 %shard_map.86.refs_1_ = bf16[16,4,128,128]{3,2,1,0:T(8,128)(2,1)} custom-call(bf16[16,4,128,128]{3,2,1,0:T(8,128)(2,1)} %get-tuple-element.18.rows_ref, bf16[16,2,128,128]{3,2,1,0:T(8,128)(2,1)} %get-tuple-element.19.keep_ref, bf16[16,2,128,128]{3,2,1,0:T(8,128)(2,1)} %collective-permute-done.1.taken_ref, ...), custom_call_target="tpu_custom_call", output_to_operand_aliasing={{}: (0, {})} | custom-call | tf_op jit(solution)/shard_map/pallas_call | solution.py:280
  79.7 0.2 collective-permute-start.2
  79.9 6.5 %all-to-all-start.2 = ((bf16[16,4,128,128]{3,2,1,0:T(8,128)(2,1)}), bf16[16,4,128,128]{3,2,1,0:T(8,128)(2,1)}, u32[]{:S(2)}, u32[]{:S(2)}) async-start(bf16[16,4,128,128]{3,2,1,0:T(8,128)(2,1)} %shard_map.86.refs_1_), calls=%async_computation.2 | async-start | bytes 4194304 | tf_op jit(solution)/shard_map/all_to_all | solution.py:420
  86.4 0.0 collective-permute-done.2.oth_ref
  86.4 21.8 %shard_map.88 = (bf16[16,3,128,128]{3,2,1,0:T(8,128)(2,1)}, bf16[16,2,128,128]{3,2,1,0:T(8,128)(2,1)}, bf16[16,2,128,128]{3,2,1,0:T(8,128)(2,1)}) custom-call(s32[24,32,32]{2,1,0:T(8,128)} %masks_ref.3, bf16[16,3,128,128]{3,2,1,0:T(8,128)(2,1)} %shard_map.87.own_ref, bf16[16,3,128,128]{3,2,1,0:T(8,128)(2,1)} %collective-permute-done.2.oth_ref), custom_call_target="tpu_custom_call" | custom-call | flops 6442450944 | bytes 8388608 | tf_op jit(solution)/shard_map/pallas_call | solution.py:211
  108.2 0.1 collective-permute-start.3
  108.3 2.8 %collective-permute-done.3.taken_ref = bf16[16,2,128,128]{3,2,1,0:T(8,128)(2,1)S(1)} collective-permute-done((bf16[16,2,128,128]{3,2,1,0:T(8,128)(2,1)}, bf16[16,2,128,128]{3,2,1,0:T(8,128)(2,1)S(1)}, u32[]{:S(2)}, u32[]{:S(2)}) %collective-permute-start.3) | collective-permute-done | bytes 1048608 | tf_op jit(solution)/shard_map/ppermute | solution.py:437
  111.2 0.0 copy-start.1
  111.2 1.0 copy-done.1
  112.1 2.4 %shard_map.89.refs_0_ = bf16[16,3,128,128]{3,2,1,0:T(8,128)(2,1)} custom-call(bf16[16,3,128,128]{3,2,1,0:T(8,128)(2,1)} %get-tuple-element.21.rows_ref, bf16[16,2,128,128]{3,2,1,0:T(8,128)(2,1)} %get-tuple-element.22.keep_ref, bf16[16,2,128,128]{3,2,1,0:T(8,128)(2,1)} %copy-done.1), custom_call_target="tpu_custom_call", output_to_operand_aliasing={{}: (0, {})} | custom-call | tf_op jit(solution)/shard_map/pallas_call | solution.py:280
  114.5 5.5 %all-to-all-done.2.refs_1_.a_ref = bf16[16,4,128,128]{3,2,1,0:T(8,128)(2,1)} async-done(((bf16[16,4,128,128]{3,2,1,0:T(8,128)(2,1)}), bf16[16,4,128,128]{3,2,1,0:T(8,128)(2,1)}, u32[]{:S(2)}, u32[]{:S(2)}) %all-to-all-start.2) | async-done | bytes 2097184 | tf_op jit(solution)/shard_map/all_to_all | solution.py:420
  120.0 3.7 %all-to-all-start.3 = ((bf16[16,3,128,128]{3,2,1,0:T(8,128)(2,1)}), bf16[16,3,128,128]{3,2,1,0:T(8,128)(2,1)S(1)}, u32[]{:S(2)}, u32[]{:S(2)}) async-start(bf16[16,3,128,128]{3,2,1,0:T(8,128)(2,1)} %shard_map.90), calls=%async_computation.3 | async-start | bytes 3145728 | tf_op jit(solution)/shard_map/all_to_all | solution.py:420
  123.7 2.6 %shard_map.91 = (bf16[128,3072]{1,0:T(8,128)(2,1)}, bf16[128,3072]{1,0:T(8,128)(2,1)}, bf16[128,3072]{1,0:T(8,128)(2,1)}, bf16[128,3072]{1,0:T(8,128)(2,1)}) custom-call(bf16[16,4,128,128]{3,2,1,0:T(8,128)(2,1)} %all-to-all-done.2.refs_1_.a_ref), custom_call_target="tpu_custom_call" | custom-call | tf_op jit(solution)/shard_map/pallas_call | solution.py:380
  126.3 21.1 %all-to-all-done.3.b_ref = bf16[16,3,128,128]{3,2,1,0:T(8,128)(2,1)S(1)} async-done(((bf16[16,3,128,128]{3,2,1,0:T(8,128)(2,1)}), bf16[16,3,128,128]{3,2,1,0:T(8,128)(2,1)S(1)}, u32[]{:S(2)}, u32[]{:S(2)}) %all-to-all-start.3) | async-done | bytes 1572896 | tf_op jit(solution)/shard_map/all_to_all | solution.py:420
  147.4 1.1 shard_map.92
  (2 shorter events, 0.0 us)
Async XLA Ops:
  40.3 4.5 %collective-permute-start = (bf16[16,4,128,128]{3,2,1,0:T(8,128)(2,1)}, bf16[16,4,128,128]{3,2,1,0:T(8,128)(2,1)}, u32[]{:S(2)}, u32[]{:S(2)}) collective-permute-start(bf16[16,4,128,128]{3,2,1,0:T(8,128)(2,1)} %all_to_all.20.own_ref), channel_id=1, source_target_pairs={{0,1},{1,0},{2,3},{3,2},{4,5},{5,4},{6,7},{7,6},{8,9},{9,8},{10,11... | collective-permute-start | bytes 6291464 | tf_op jit(solution)/shard_map/ppermute | solution.py:430
  40.3 34.1 %all-to-all-start = ((bf16[16,3,128,128]{3,2,1,0:T(8,128)(2,1)}), bf16[16,3,128,128]{3,2,1,0:T(8,128)(2,1)S(1)}, u32[]{:S(2)}, u32[]{:S(2)}) async-start(bf16[16,3,128,128]{3,2,1,0:T(8,128)(2,1)} %get-tuple-element.16), calls=%async_computation | async-start | bytes 3145728 | tf_op jit(solution)/shard_map/all_to_all | solution.py:420
  74.2 3.1 %collective-permute-start.1 = (bf16[16,2,128,128]{3,2,1,0:T(8,128)(2,1)}, bf16[16,2,128,128]{3,2,1,0:T(8,128)(2,1)}, u32[]{:S(2)}, u32[]{:S(2)}) collective-permute-start(bf16[16,2,128,128]{3,2,1,0:T(8,128)(2,1)} %get-tuple-element.20), channel_id=1, source_target_pairs={{0,1},{1,0},{2,3},{3,2},{4,5},{5,4},{6,7},{7,6},{8,9},{9,8},{10,11... | collective-permute-start | bytes 3145736 | tf_op jit(solution)/shard_map/ppermute | solution.py:424
  74.4 2.9 %copy-start = (bf16[16,3,128,128]{3,2,1,0:T(8,128)(2,1)}, bf16[16,3,128,128]{3,2,1,0:T(8,128)(2,1)S(1)}, u32[]{:S(2)}) copy-start(bf16[16,3,128,128]{3,2,1,0:T(8,128)(2,1)S(1)} %all-to-all-done.refs_0_) | copy-start | bytes 4718596
  79.7 6.8 %collective-permute-start.2 = (bf16[16,3,128,128]{3,2,1,0:T(8,128)(2,1)}, bf16[16,3,128,128]{3,2,1,0:T(8,128)(2,1)}, u32[]{:S(2)}, u32[]{:S(2)}) collective-permute-start(bf16[16,3,128,128]{3,2,1,0:T(8,128)(2,1)} %shard_map.87.own_ref), channel_id=1, source_target_pairs={{0,1},{1,0},{2,3},{3,2},{4,5},{5,4},{6,7},{7,6},{8,9},{9,8},{10,11... | collective-permute-start | bytes 4718600 | tf_op jit(solution)/shard_map/ppermute | solution.py:433
  79.9 40.1 %all-to-all-start.2 = ((bf16[16,4,128,128]{3,2,1,0:T(8,128)(2,1)}), bf16[16,4,128,128]{3,2,1,0:T(8,128)(2,1)}, u32[]{:S(2)}, u32[]{:S(2)}) async-start(bf16[16,4,128,128]{3,2,1,0:T(8,128)(2,1)} %shard_map.86.refs_1_), calls=%async_computation.2 | async-start | bytes 4194304 | tf_op jit(solution)/shard_map/all_to_all | solution.py:420
  108.2 3.0 %collective-permute-start.3 = (bf16[16,2,128,128]{3,2,1,0:T(8,128)(2,1)}, bf16[16,2,128,128]{3,2,1,0:T(8,128)(2,1)S(1)}, u32[]{:S(2)}, u32[]{:S(2)}) collective-permute-start(bf16[16,2,128,128]{3,2,1,0:T(8,128)(2,1)} %get-tuple-element.23), channel_id=1, source_target_pairs={{0,1},{1,0},{2,3},{3,2},{4,5},{5,4},{6,7},{7,6},{8,9},{9,8},{10,11... | collective-permute-start | bytes 3145736 | tf_op jit(solution)/shard_map/ppermute | solution.py:437
  111.2 1.0 copy-start.1
  120.0 27.4 %all-to-all-start.3 = ((bf16[16,3,128,128]{3,2,1,0:T(8,128)(2,1)}), bf16[16,3,128,128]{3,2,1,0:T(8,128)(2,1)S(1)}, u32[]{:S(2)}, u32[]{:S(2)}) async-start(bf16[16,3,128,128]{3,2,1,0:T(8,128)(2,1)} %shard_map.90), calls=%async_computation.3 | async-start | bytes 3145728 | tf_op jit(solution)/shard_map/all_to_all | solution.py:420
